TPU v7x, 128 devices: a whole 4x4x4 slice. The times are simulated.
128 devices in a mesh: dp: 4 (over z), ctx: 32 (over y, x, core).
Axes of the slice: x: 4, y: 4, z: 4, core: 2. Of those that a mesh axis runs over, the one named last changes fastest.
Arguments:
- queries: bfloat16 [4, 4096, 1024], P('dp', 'ctx'), may hold values from -6 to 6
- key_in: bfloat16 [4, 4096, 1024], P('dp', 'ctx'), may hold values from -6 to 6
- value_in: bfloat16 [4, 4096, 2048], P('dp', 'ctx'), may hold values from -6 to 6
- gate_in: bfloat16 [4, 4096, 2048], P('dp', 'ctx'), may hold values from -6 to 6
- residual_in: bfloat16 [4, 4096, 2048], P('dp', 'ctx'), may hold values from -6 to 6
- log_decay: float32 [4, 16, 4096], P('dp', None, 'ctx'), may hold values from -1 to 0
- beta_logit: float32 [4, 16, 4096], P('dp', None, 'ctx'), may hold values from -6 to 6
- lengths: int32 [4, 4], P('dp'), may hold values from 1 to 2048, 4096 in all within a row
- head_gain: float32 [128], replicated, may hold values from 0.1 to 1.9
- out_proj: bfloat16 [2048, 2048], replicated, may hold values from -0.125 to 0.125
- post_gain: float32 [2048], replicated, may hold values from 0.1 to 1.9
- expert_in: bfloat16 [256, 2048, 1024], P(('dp', 'ctx')), may hold values from -0.125 to 0.125
- expert_out: bfloat16 [256, 512, 2048], P(('dp', 'ctx')), may hold values from -0.25 to 0.25
- routes: int32 [4, 4096, 10], P('dp', 'ctx'), may hold values from 0 to 255, all different within a row; in each aligned block of 128 rows (0 to 127, 128 to 255, ..., all dimensions but the last counted through in order) at most 6 rows name the same one
- route_gates: float32 [4, 4096, 10], P('dp', 'ctx'), may hold values from 0.05 to 0.25
Outputs:
- layer_out: bfloat16 [4, 4096, 2048], P('dp', 'ctx')
Inputs may be any that keep to these rules, and one draw needn't show every extreme that they name: `routes`: each row names 10 different experts; among the rows of one device (aligned blocks of 128 positions) no expert is named more than 6 times, a bound that some block reaches. The lengths of a pack sum to 4096.
All inputs are finite; a program needn't handle non-finite values.
Results may differ from a plain program's by a relative error of at most 0.014.
Values may be sent and summed in bfloat16 or wider, within the bound.
No kernel may reach another device: no remote copies, remote signals or barrier semaphores. Data moves between devices by JAX's collectives and lax.ppermute only.
A program may use at most 256 MiB of HBM per device.

v0:
```python
import jax
import jax.numpy as jnp
from jax import lax
from jax.sharding import PartitionSpec as P

D = 2048
DK = 128
DV = 128
FF = 512
TOPK = 10
HK = 8
HV = 16
BLOCK = 64


EPSILON = 1e-06
HIGHEST = lax.Precision.HIGHEST
ROWWISE = lax.Precision.HIGH


def entering(part, axis, combine, identity):
    place = lax.axis_index(axis)
    gathered = jax.tree.map(lambda a: lax.all_gather(a, axis), part)
    state = jax.tree.map(lambda a, e: jnp.zeros_like(a) + jnp.asarray(e, a.dtype), part, identity)

    def one(lap, state):
        return combine(
            state, jax.tree.map(lambda a: lax.dynamic_index_in_dim(a, lap, 0, False), gathered)
        )

    return lax.fori_loop(0, place, one, state)


def unit_heads(matrix, head_count, factor):
    shaped = matrix.astype(jnp.float32).reshape(matrix.shape[0], head_count, -1)
    return shaped * lax.rsqrt(jnp.sum(shaped * shaped, -1, keepdims=True) + EPSILON) * factor


def segment_of(lengths, positions):
    starts = jnp.cumsum(lengths) - lengths
    return jnp.sum((starts[:, None] <= positions[None, :]).astype(jnp.int32), 0) - 1


def block_terms(queries, key_rows, value_rows, beta_gate, decay_log, segment, seg_before):
    length = key_rows.shape[1]
    cumulative = jnp.cumsum(decay_log, axis=-1)
    rows_at = jnp.arange(length)[:, None]
    cols_at = jnp.arange(length)[None, :]
    same_doc = (segment[:, None] == segment[None, :]) & (rows_at >= cols_at)
    log_gap = jnp.minimum(cumulative[:, :, None] - cumulative[:, None, :], 0.0)
    decay_pair = jnp.where(same_doc[None], jnp.exp(log_gap), 0.0)
    from_start = jnp.where((segment == seg_before)[None, :], jnp.exp(cumulative), 0.0)
    to_end = decay_pair[:, -1, :]
    key_inner = jnp.einsum("hcd,hsd->hcs", key_rows, key_rows, precision=ROWWISE)
    lower_part = jnp.where(
        (rows_at > cols_at)[None], beta_gate[:, :, None] * decay_pair * key_inner, 0.0
    )
    system = jnp.eye(length, dtype=jnp.float32)[None] + lower_part
    right_side = jnp.concatenate(
        [beta_gate[:, :, None] * value_rows, (beta_gate * from_start)[:, :, None] * key_rows],
        axis=-1,
    )
    solved = jax.scipy.linalg.solve_triangular(system, right_side, lower=True, unit_diagonal=True)
    value_width = value_rows.shape[-1]
    pseudo = solved[..., :value_width]
    weights = solved[..., value_width:]
    scores = jnp.einsum("hcd,hsd->hcs", queries, key_rows, precision=ROWWISE) * decay_pair
    weighted = key_rows * to_end[:, :, None]
    key_width = key_rows.shape[-1]
    transition = from_start[:, -1][:, None, None] * jnp.eye(key_width, dtype=jnp.float32)[
        None
    ] - jnp.einsum("hcd,hce->hde", weighted, weights, precision=HIGHEST)
    offset = jnp.einsum("hcd,hce->hde", weighted, pseudo, precision=HIGHEST)
    return (pseudo, weights, scores, from_start, transition, offset)


def block_output(queries, pseudo, weights, scores, from_start, carried):
    errors = pseudo - jnp.einsum("hcd,hde->hce", weights, carried, precision=ROWWISE)
    return jnp.einsum(
        "hcd,hde->hce", queries * from_start[:, :, None], carried, precision=ROWWISE
    ) + jnp.einsum("hcs,hse->hce", scores, errors, precision=ROWWISE)


def apply_map(transition, carried):
    return jnp.einsum("hde,hef->hdf", transition, carried, precision=HIGHEST)


def head_blocks(matrix, block_len):
    length, head_count, inner_width = matrix.shape
    return matrix.reshape(length // block_len, block_len, head_count, inner_width).transpose(
        0, 2, 1, 3
    )


def prepare(queries, key_in, value_in, log_decay, beta_logit, segment, seg_before):
    length = queries.shape[0]
    group_size = HV // HK
    query_heads = jnp.repeat(unit_heads(queries, HK, DK ** (-0.5)), group_size, axis=1)
    key_heads = jnp.repeat(unit_heads(key_in, HK, 1.0), group_size, axis=1)
    value_heads = value_in.astype(jnp.float32).reshape(length, HV, DV)
    nblock = length // BLOCK
    beta_gate = jax.nn.sigmoid(beta_logit).reshape(HV, nblock, BLOCK).transpose(1, 0, 2)
    decay_log = log_decay.reshape(HV, nblock, BLOCK).transpose(1, 0, 2)
    seg_blocks = segment.reshape(nblock, BLOCK)
    seg_starts = jnp.concatenate([jnp.reshape(seg_before, (1,)), seg_blocks[:-1, -1]])
    query_blocks = head_blocks(query_heads, BLOCK)
    terms = jax.vmap(block_terms)(
        query_blocks,
        head_blocks(key_heads, BLOCK),
        head_blocks(value_heads, BLOCK),
        beta_gate,
        decay_log,
        seg_blocks,
        seg_starts,
    )
    return (query_blocks, terms)


def finish(query_blocks, terms, start_state, gate_in, residual_in, head_gain, out_proj):
    pseudo, weights, scores, from_start, transition, offset = terms

    def advance(carried, member):
        return (apply_map(member[0], carried) + member[1], carried)

    final_state, block_starts = lax.scan(advance, start_state, (transition, offset))
    outputs = jax.vmap(block_output)(
        query_blocks, pseudo, weights, scores, from_start, block_starts
    )
    length = gate_in.shape[0]
    outputs = outputs.transpose(0, 2, 1, 3).reshape(length, HV, DV)
    mean_square = jnp.mean(outputs * outputs, -1, keepdims=True)
    gate_heads = gate_in.astype(jnp.float32).reshape(length, HV, DV)
    normed = (
        (outputs * lax.rsqrt(mean_square + EPSILON) * head_gain * jax.nn.silu(gate_heads))
        .reshape(length, HV * DV)
        .astype(jnp.bfloat16)
    )
    mixed = jnp.dot(normed, out_proj, preferred_element_type=jnp.float32)
    return (residual_in.astype(jnp.float32) + mixed).astype(jnp.bfloat16)


def post_norm(hidden_state, post_gain):
    widened = hidden_state.astype(jnp.float32)
    return (
        widened * lax.rsqrt(jnp.mean(widened * widened, -1, keepdims=True) + EPSILON) * post_gain
    ).astype(jnp.bfloat16)


def rank_of(flat_ids, experts):
    onehot = (flat_ids[:, None] == jnp.arange(experts, dtype=jnp.int32)[None, :]).astype(jnp.int32)
    return jnp.sum((jnp.cumsum(onehot, 0) - onehot) * onehot, 1)


def expert_apply(routed, expert_in, expert_out):
    gate_up = jnp.einsum("sjcd,jdf->sjcf", routed, expert_in, preferred_element_type=jnp.float32)
    hidden_units = (jax.nn.silu(gate_up[..., :FF]) * gate_up[..., FF:]).astype(jnp.bfloat16)
    return jnp.einsum(
        "sjcf,jfd->sjcd", hidden_units, expert_out, preferred_element_type=jnp.float32
    ).astype(jnp.bfloat16)


def per_device(
    queries,
    key_in,
    value_in,
    gate_in,
    residual_in,
    log_decay,
    beta_logit,
    lengths,
    head_gain,
    out_proj,
    post_gain,
    expert_in,
    expert_out,
    routes,
    route_gates,
):
    tokens_dev = queries.shape[1]
    ctx_index = lax.axis_index("ctx")
    positions = ctx_index * tokens_dev + jnp.arange(tokens_dev, dtype=jnp.int32)
    segment = segment_of(lengths[0], positions)
    previous = segment_of(lengths[0], jnp.reshape(positions[0] - 1, (1,)))[0]
    seg_before = jnp.where(ctx_index > 0, previous, -1)
    query_blocks, terms = prepare(
        queries[0], key_in[0], value_in[0], log_decay[0], beta_logit[0], segment, seg_before
    )
    eye_maps = jnp.broadcast_to(jnp.eye(DK, dtype=jnp.float32), (HV, DK, DK))
    zero_offset = jnp.zeros((HV, DK, DV), jnp.float32)

    def compose(carry_pair, member):
        return (
            (apply_map(member[0], carry_pair[0]), apply_map(member[0], carry_pair[1]) + member[1]),
            None,
        )

    device_pair, unused = lax.scan(compose, (eye_maps, zero_offset), (terms[4], terms[5]))

    def combine(earlier, later):
        return (apply_map(later[0], earlier[0]), apply_map(later[0], earlier[1]) + later[1])

    prefix_map, prefix_offset = entering(
        (device_pair[0], device_pair[1]), "ctx", combine, (eye_maps, zero_offset)
    )
    hidden_state = finish(
        query_blocks, terms, prefix_offset, gate_in[0], residual_in[0], head_gain, out_proj
    )
    expert_input = post_norm(hidden_state, post_gain)
    local_experts = expert_in.shape[0]
    device_count = lax.axis_size("dp") * lax.axis_size("ctx")
    experts_all = local_experts * device_count
    capacity = tokens_dev * TOPK * 6 // (5 * experts_all)
    flat_ids = routes[0].reshape(-1)
    slot_rank = rank_of(flat_ids, experts_all)
    outbound = (
        jnp.zeros((experts_all, capacity, D), jnp.bfloat16)
        .at[flat_ids, slot_rank]
        .set(jnp.repeat(expert_input, TOPK, axis=0))
    )
    outbound = outbound.reshape(device_count, local_experts, capacity, D)
    computed = expert_apply(
        lax.all_to_all(outbound, ("dp", "ctx"), split_axis=0, concat_axis=0, tiled=True),
        expert_in,
        expert_out,
    )
    returned = lax.all_to_all(computed, ("dp", "ctx"), split_axis=0, concat_axis=0, tiled=True)
    back_rows = returned.reshape(experts_all, capacity, D)[flat_ids, slot_rank]
    expert_mix = jnp.sum(
        back_rows.astype(jnp.float32).reshape(tokens_dev, TOPK, D) * route_gates[0][:, :, None], 1
    )
    summed = hidden_state.astype(jnp.float32) + expert_mix
    return summed.astype(jnp.bfloat16)[None]


def solution(mesh):
    in_specs = (
        P("dp", "ctx", None),
        P("dp", "ctx", None),
        P("dp", "ctx", None),
        P("dp", "ctx", None),
        P("dp", "ctx", None),
        P("dp", None, "ctx"),
        P("dp", None, "ctx"),
        P("dp", None),
        P(),
        P(),
        P(),
        P(("dp", "ctx"), None, None),
        P(("dp", "ctx"), None, None),
        P("dp", "ctx", None),
        P("dp", "ctx", None),
    )
    out_specs = P("dp", "ctx", None)
    return jax.shard_map(
        per_device, mesh=mesh, in_specs=in_specs, out_specs=out_specs, check_vma=False
    )
```

profile of v0, /device:TPU:1, one launch (start us, length us, event | category | flops | bytes accessed | tf_op | source)
XLA Modules:
  0.0 862.9 jit_solution(10262257200159182205)
XLA Ops:
  6.6 0.9 reduce-window.10
  7.5 0.7 bitcast_subtract_fusion.1
  8.2 1.4 fusion.78
  9.8 0.6 slice.37
  11.0 0.6 pad_add_fusion.1
  11.7 0.8 reshape_squeeze.6
  12.5 0.7 add_divide_fusion
  13.2 1.0 convert_bitcast_fusion.2
  15.9 1.3 exponential_select_fusion
  17.3 2.1 fusion.44
  19.4 158.1 %custom-call.4 = f32[2,16,1,64,64]{3,4,2,1,0:T(8,128)S(1)} custom-call(f32[2,16,1,64,64]{4,3,2,1,0:T(8,128)} %fusion.44), custom_call_target="InvertDiagBlocksLowerTriangular" | custom-call | tf_op jit(solution)/shard_map/vmap(jit(_solve_triangular))/vmap()/triangular_solve | solution.py:63
  177.7 0.9 slice.49
  178.6 0.6 bitcast_multiply_fusion.1
  179.2 2.0 fusion.31
  181.3 5.1 fusion.60
  186.4 4.0 multiply_subtract_fusion
  190.5 12.0 %while.39 = (s32[]{:T(128)}, f32[16,128,128]{2,1,0:T(8,128)S(1)}, f32[16,128,128]{2,1,0:T(8,128)}, f32[2,16,128,128]{3,2,1,0:T(8,128)S(1)}, f32[2,16,128,128]{3,2,1,0:T(8,128)}, /*index=5*/s32[]{:T(128)}, s32[]{:T(128)}) while((s32[]{:T(128)}, f32[16,128,128]{2,1,0:T(8,128)S(1)}, f32[16,128,128]{2,1,0:T(8,128)}, ...), condition=%wide.region_7.8_spmd.clone, body=%wide.region_6.7_spmd.clone.sunk | while | flops 805830656 | bytes 11535451 | solution.py:197
  190.8 1.2 copy.215
  192.0 3.3 convolution_add_fusion.10
  195.4 1.2 fusion.108
  196.6 1.2 copy.215
  197.9 3.3 convolution_add_fusion.10
  201.3 1.2 fusion.108
  202.5 1.0 copy-done.3
  203.6 0.7 all-gather.7.cloned.1.call-update
  206.0 1.3 copy-done.9
  207.4 1.8 broadcast_add_fusion
  209.2 0.8 copy.121
  210.0 0.5 fusion.46
  210.8 1.0 copy-done.7
  211.8 2.0 convolution_multiply_fusion
  213.8 107.2 %all-gather.5.cloned.1.call-done = f32[512,128,128]{2,1,0:T(8,128)} async-done(((f32[16,128,128]{2,1,0:T(8,128)}), f32[512,128,128]{2,1,0:T(8,128)}) %all-gather.5.cloned.1.call-update) | async-done | bytes 33554448 | tf_op jit(solution)/shard_map/all_gather | solution.py:23
  321.0 115.3 %all-gather.7.cloned.1.call-done = f32[512,128,128]{2,1,0:T(8,128)} async-done(((f32[16,128,128]{2,1,0:T(8,128)}), f32[512,128,128]{2,1,0:T(8,128)}) %all-gather.7.cloned.1.call-update) | async-done | bytes 33554448 | tf_op jit(solution)/shard_map/all_gather | solution.py:23
  436.4 2.9 while.37
  436.6 2.8 convolution_add_fusion.8
  439.3 6.7 while.38
  439.7 1.1 bitcast_dynamic-update-slice_fusion.2
  440.8 0.8 copy-done.2
  441.6 1.2 convolution_add_fusion.9
  442.9 1.1 bitcast_dynamic-update-slice_fusion.2
  444.0 0.7 copy-done.2
  444.8 1.2 convolution_add_fusion.9
  446.0 3.3 convolution_subtract_fusion
  449.4 1.0 fusion.56
  450.6 0.9 multiply_reduce_fusion.2
  451.6 0.6 copy.114
  452.6 5.5 multiply_reduce_fusion.1
  458.3 4.4 broadcast_in_dim.62
  462.7 9.8 %reshape.296 = bf16[1280,2048]{1,0:T(8,128)(2,1)} reshape(bf16[128,10,2048]{2,1,0:T(8,128)(2,1)} %broadcast_in_dim.62) | data formatting | bytes 10485760 | tf_op jit(solution)/shard_map/reshape | solution.py:218
  472.5 15.0 %scatter_custom_fusion = bf16[1536,2048]{1,0:T(8,128)(2,1)} fusion(s32[1280]{0:T(1024)S(1)} %broadcast_select_fusion, bf16[1280,2048]{1,0:T(8,128)(2,1)} %reshape.296, bf16[]{:T(256)} %constant.92.clone.1), kind=kCustom, calls=%fused_computation.31 | custom fusion | bytes 6291968
  487.5 10.9 %reshape.276 = bf16[128,2,6,2048]{3,1,0,2:T(2,128)(2,1)} reshape(bf16[256,6,2048]{2,0,1:T(8,128)(2,1)} %bitcast.184) | data formatting | bytes 12582912 | tf_op jit(solution)/shard_map/reshape | solution.py:220
  498.4 8.2 copy.122
  506.6 168.5 %all_to_all.10 = bf16[128,2,6,2048]{3,1,2,0:T(2,128)(2,1)S(1)} all-to-all(bf16[128,2,6,2048]{3,1,2,0:T(2,128)(2,1)S(1)} %copy.122), channel_id=1, replica_groups=mesh['dp'=4,'ctx'=32] {'dp','ctx'}, dimensions={0} | all-to-all | bytes 12582912 | tf_op jit(solution)/shard_map/all_to_all | solution.py:222
  675.1 12.9 %fusion.24 = f32[128,2,6,1024]{3,0,2,1:T(8,128)} fusion(bf16[2,2048,1024]{2,1,0:T(8,128)(2,1)S(1)} %bitcast.204, bf16[128,2,6,2048]{3,1,2,0:T(2,128)(2,1)S(1)} %all_to_all.10), kind=kOutput, calls=%fused_computation.33 | convolution fusion | flops 6442450944 | bytes 20971520 | tf_op jit(solution)/shard_map/sjcd,jdf->sjcf/dot_general | solution.py:155
  688.1 6.6 convert_bitcast_fusion
  694.7 17.9 %copy.124 = bf16[128,2,6,2048]{3,1,2,0:T(2,128)(2,1)} copy(bf16[128,2,6,2048]{3,0,2,1:T(8,128)(2,1)S(1)} %convert_bitcast_fusion) | data formatting | bytes 12582912 | tf_op jit(solution)/shard_map/convert_element_type | solution.py:159
  712.6 6.0 all-to-all-start.1
  718.8 75.1 %all-to-all-done.1 = bf16[128,2,6,2048]{3,1,2,0:T(2,128)(2,1)} async-done(((bf16[128,2,6,2048]{3,1,2,0:T(2,128)(2,1)}), bf16[128,2,6,2048]{3,1,2,0:T(2,128)(2,1)}, u32[]{:S(2)}, u32[]{:S(2)}) %all-to-all-start.1) | async-done | bytes 6291488 | tf_op jit(solution)/shard_map/all_to_all | solution.py:226
  793.9 6.8 copy.125
  800.6 10.2 %reshape.277 = bf16[256,6,2048]{2,0,1:T(8,128)(2,1)} reshape(bf16[128,2,6,2048]{3,1,0,2:T(2,128)(2,1)} %copy.125) | data formatting | bytes 12582912 | tf_op jit(solution)/shard_map/reshape | solution.py:227
  810.8 24.1 %gather_fusion = bf16[1280,2048]{1,0:T(8,128)(2,1)} fusion(bf16[256,6,2048]{2,0,1:T(8,128)(2,1)} %reshape.277, s32[1280]{0:T(1024)S(1)} %get-tuple-element.156), kind=kCustom, calls=%fused_computation | custom fusion | bytes 10496000 | tf_op jit(solution)/shard_map/gather | solution.py:227
  834.9 10.4 %reshape.286 = f32[128,10,2048]{2,1,0:T(8,128)} reshape(bf16[1280,2048]{1,0:T(8,128)(2,1)} %gather_fusion) | data formatting | bytes 15728640 | tf_op jit(solution)/shard_map/convert_element_type | solution.py:229
  845.3 9.6 %multiply_reduce_fusion = f32[128,2048]{1,0:T(8,128)S(1)} fusion(f32[128,10,2048]{2,1,0:T(8,128)} %reshape.286, f32[128,10]{1,0:T(8,128)S(1)} %bitcast.194), kind=kLoop, calls=%fused_computation.23 | loop fusion | flops 4980736 | bytes 11539456 | tf_op jit(solution)/shard_map/reduce_sum | solution.py:228
  854.9 0.9 fusion.69
  (110 shorter events, 5.8 us)
Async XLA Ops:
  6.5 204.2 %copy-start = (f32[128]{0:T(128)S(1)}, f32[128]{0:T(128)}, u32[]{:S(2)}) copy-start(f32[128]{0:T(128)} %param.29) | copy-start | bytes 1540
  6.5 8.4 copy-start.12
  6.5 314.5 %all-gather.5.cloned.1.call-start = ((), (), s32[]{:S(2)}) async-start(), calls=%async_computation.2 | async-start | bytes 34603008 | tf_op jit(solution)/shard_map/all_gather | solution.py:23
  17.3 169.1 %copy-start.4 = (f32[128,8,2,128]{3,0,2,1:T(8,128)}, f32[128,8,2,128]{3,0,2,1:T(8,128)S(1)}, u32[]{:S(2)}) copy-start(f32[128,8,2,128]{3,0,2,1:T(8,128)S(1)} %broadcast_in_dim.57) | copy-start | bytes 3145732
  181.3 9.1 %copy-start.6 = (f32[2,16,64,256]{3,2,1,0:T(8,128)}, f32[2,16,64,256]{3,2,1,0:T(8,128)S(1)}, u32[]{:S(2)}) copy-start(f32[2,16,64,256]{3,2,1,0:T(8,128)S(1)} %fusion.31) | copy-start | bytes 6291460
  190.5 13.8 %copy-start.15 = (s32[1,128,10]{1,0,2:T(1,128)S(1)}, s32[1,128,10]{1,0,2:T(1,128)}, u32[]{:S(2)}) copy-start(s32[1,128,10]{1,0,2:T(1,128)} %param.34) | copy-start | bytes 15364
  190.5 14.3 %copy-start.13 = (bf16[1,128,1024]{2,1,0:T(8,128)(2,1)S(1)}, bf16[1,128,1024]{2,1,0:T(8,128)(2,1)}, u32[]{:S(2)}) copy-start(bf16[1,128,1024]{2,1,0:T(8,128)(2,1)} %param.21) | copy-start | bytes 786436
  202.5 1.0 copy-start.3
  203.5 232.8 %all-gather.7.cloned.1.call-start = ((), (), s32[]{:S(2)}) async-start(), calls=%async_computation.3 | async-start | bytes 34603008 | tf_op jit(solution)/shard_map/all_gather | solution.py:23
  206.0 1.3 copy-start.9
  209.2 1.3 copy-start.18
  209.2 1.4 copy-start.17
  209.2 2.6 copy-start.5
  210.8 1.0 copy-start.7
  439.6 2.0 copy-start.2
  442.8 2.0 copy-start.2
  446.0 3.3 copy-start.8
  446.0 3.3 copy-start.10
  449.4 1.2 copy-start.11
  450.6 2.0 copy-start.20
  450.6 2.0 copy-start.21
  452.6 5.5 copy-start.14
  498.4 176.7 %slice-start = ((s8[8388608]{0:T(1024)(128)(4,1)}), s8[4194304]{0:T(1024)(128)(4,1)S(1)}, s32[]{:S(2)}) async-start(s8[8388608]{0:T(1024)(128)(4,1)} %bitcast.203), calls=%async_computation.4 | async-start | bytes 8388608
  506.6 168.5 %slice-start.1 = ((s8[8388608]{0:T(1024)(128)(4,1)}), s8[4194304]{0:T(1024)(128)(4,1)S(1)}, s32[]{:S(2)}) async-start(s8[8388608]{0:T(1024)(128)(4,1)} %bitcast.203), calls=%async_computation.5 | async-start | bytes 8388608
  675.1 13.0 %copy-start.19 = (bf16[2,512,2048]{2,1,0:T(8,128)(2,1)S(1)}, bf16[2,512,2048]{2,1,0:T(8,128)(2,1)}, u32[]{:S(2)}) copy-start(bf16[2,512,2048]{2,1,0:T(8,128)(2,1)} %param.33) | copy-start | bytes 12582916
  712.6 6.0 copy-start.16
  712.6 81.3 %all-to-all-start.1 = ((bf16[128,2,6,2048]{3,1,2,0:T(2,128)(2,1)}), bf16[128,2,6,2048]{3,1,2,0:T(2,128)(2,1)}, u32[]{:S(2)}, u32[]{:S(2)}) async-start(bf16[128,2,6,2048]{3,1,2,0:T(2,128)(2,1)} %copy.124), calls=%async_computation.1 | async-start | bytes 12582912 | tf_op jit(solution)/shard_map/all_to_all | solution.py:226
  845.3 10.5 %copy-start.1 = (f32[128]{0:T(128)S(1)}, f32[128]{0:T(128)}, u32[]{:S(2)}) copy-start(f32[128]{0:T(128)} %param.29) | copy-start | bytes 1540
Sparse Core Ops, SparseCore 0:
  203.7 117.3 all-gather.4
  323.3 113.0 all-gather.6
where the time goes:
time: 869 us; the launch traced here: 863 us
  waiting for transfers between devices  298 us (34%)
  other arithmetic  181 us (21%)
  blocking collectives  168 us (19%)
  local copies, waits for them, and re-layouts  134 us (15%)
  matrix products  59.7 us (7%)
  between operations  15 us (2%)
    all_gather x2, waiting for transfers between devices, entering(): gathered = jax.tree.map(lambda a: lax.all_gather(a, axis), part)  223 us
    all_to_all x1, blocking collectives, per_device(): lax.all_to_all(outbound, ('dp', 'ctx'), split_axis=0, concat_axis=0, tile...  168 us
    another operation x2, other arithmetic, block_terms(): jax.scipy.linalg.solve_triangular(system, right_side, lower=True, unit_di...  158 us
    all_to_all x1, waiting for transfers between devices, per_device(): lax.all_to_all(computed, ('dp', 'ctx'), split_axis=0, concat_axis=0, tile...  75.1 us
    gather x1, local copies, waits for them, and re-layouts, per_device(): back_rows = returned.reshape(experts_all, capacity, D)[flat_ids, slot_rank]  24.1 us
    reshape x2, local copies, waits for them, and re-layouts, per_device(): outbound = outbound.reshape(device_count, local_experts, capacity, D)  19.1 us
    unnamed x51, local copies, waits for them, and re-layouts  19 us
    convert_element_type x1, local copies, waits for them, and re-layouts, expert_apply(): return jnp.einsum('sjcf,jfd->sjcd', hidden_units, expert_out, preferred_e...  17.9 us
  transfers between devices with their start and end apart: 3, of which 3 were waited for; matrix products, arithmetic and copies ran while one was open for 1% of the time, Pallas kernels for 0%

commit v1 on v0

v1 whole, which is shorter than its diff:
```python
import functools

import jax
import jax.numpy as jnp
from jax import lax
from jax.experimental import pallas as pl
from jax.experimental.pallas import tpu as pltpu
from jax.sharding import PartitionSpec as P

D = 2048
DK = 128
DV = 128
FF = 512
TOPK = 10
HK = 8
HV = 16
TOK = 128
CAP = 6
GROUPS = 4
WIDTH = D // GROUPS
SPAN = GROUPS * CAP
EPSILON = 1e-06

F32 = jnp.float32
BF16 = jnp.bfloat16
HEADS_STEP = 8
MAP_ROWS = 64 + 128 + 16
SRC_GROUP = 8
GROUP_ROWS = SRC_GROUP * SPAN
PIECE = SRC_GROUP * CAP
MIB = 1 << 20


def dot_nn(a, b):
    return lax.dot_general(a, b, (((1,), (0,)), ((), ())), preferred_element_type=F32)


def dot_nt(a, b):
    return lax.dot_general(a, b, (((1,), (1,)), ((), ())), preferred_element_type=F32)


def halves(x):
    high = x.astype(BF16)
    return high, (x - high.astype(F32)).astype(BF16)


def wide(x):
    high, low = halves(x)
    return jnp.concatenate([high, low], axis=1)


def twice(x, axis):
    return jnp.concatenate([x, x], axis=axis)


def iota(shape, axis):
    return lax.broadcasted_iota(jnp.int32, shape, axis)


def params(limit=48 * MIB):
    return pltpu.CompilerParams(vmem_limit_bytes=limit)


def mixer_kernel(
    len_ref, q_ref, k_ref, v_ref, decay_ref, beta_ref, maps_ref, query_ref, local_ref
):
    first = lax.axis_index("ctx") * TOK
    start1 = len_ref[0, 0]
    start2 = start1 + len_ref[0, 1]
    start3 = start2 + len_ref[0, 2]

    def segment(at):
        return (
            (at >= 0).astype(jnp.int32)
            + (at >= start1).astype(jnp.int32)
            + (at >= start2).astype(jnp.int32)
            + (at >= start3).astype(jnp.int32)
        )

    square = (TOK, TOK)
    rows, cols = iota(square, 0), iota(square, 1)
    seg_rows, seg_cols = segment(first + rows), segment(first + cols)
    seg_before, seg_last = segment(first - 1), segment(first + TOK - 1)
    lower = (seg_rows == seg_cols) & (rows >= cols)
    strict = rows > cols
    diagonal = rows == cols
    eye = diagonal.astype(F32)
    eye_bf = eye.astype(BF16)
    pair_masks = {}
    size = 1
    while size < TOK:
        pair_masks[size] = (rows // (2 * size) == cols // (2 * size)) & (
            rows // size != cols // size
        )
        size *= 2

    heads = range(HEADS_STEP)
    keys = range(HEADS_STEP // 2)
    upper = (rows <= cols).astype(F32)
    cum_row = lax.dot_general(
        decay_ref[...],
        upper,
        (((1,), (0,)), ((), ())),
        precision=lax.Precision.HIGHEST,
        preferred_element_type=F32,
    )
    beta_row = 1.0 / (1.0 + jnp.exp(-beta_ref[...]))
    columns = jnp.concatenate(
        [cum_row, beta_row, jnp.zeros((TOK - 2 * HEADS_STEP, TOK), F32)], axis=0
    ).T
    row8 = iota((HEADS_STEP, TOK), 1)
    enter_row = jnp.where(segment(first + row8) == seg_before, jnp.exp(cum_row), 0.0)
    col_at = iota((TOK, 1), 0)
    enters = segment(first + col_at) == seg_before
    leaves = segment(first + col_at) == seg_last

    key = [k_ref[:, i * DK : (i + 1) * DK] for i in keys]
    query = [q_ref[:, i * DK : (i + 1) * DK] for i in keys]
    key_t = [k.T for k in key]
    inner = [dot_nt(k, k) for k in key]
    cross = [dot_nt(q, k) for q, k in zip(query, key)]
    inner_diag = [jnp.where(diagonal, x, 0.0) for x in inner]
    key_row = [lax.rsqrt(jnp.sum(x, 0, keepdims=True) + EPSILON) for x in inner_diag]
    key_col = [lax.rsqrt(jnp.sum(x, 1, keepdims=True) + EPSILON) for x in inner_diag]
    query_f = [q.astype(F32) for q in query]
    query_col = [
        lax.rsqrt(jnp.sum(q * q, 1, keepdims=True) + EPSILON) * (DK**-0.5) for q in query_f
    ]
    inner = [x * r for x, r in zip(inner, key_row)]
    cross = [x * r * c for x, r, c in zip(cross, key_row, query_col)]

    cum_col = [columns[:, h : h + 1] for h in heads]
    beta_col = [columns[:, HEADS_STEP + h : HEADS_STEP + h + 1] for h in heads]
    decay = [
        jnp.where(lower, jnp.exp(jnp.minimum(cum_col[h] - cum_row[h : h + 1], 0.0)), 0.0)
        for h in heads
    ]
    system = [
        jnp.where(strict, (beta_col[h] * key_col[h // 2]) * decay[h] * inner[h // 2], 0.0)
        for h in heads
    ]
    system_bf = [x.astype(BF16) for x in system]
    zero_bf = jnp.zeros(square, BF16)
    inverse = [eye_bf - jnp.where(pair_masks[1], x, zero_bf) for x in system_bf]
    size = 2
    while size < TOK:
        mask = pair_masks[size]
        inside = [
            dot_nn(jnp.where(mask, system_bf[h], zero_bf), inverse[h]).astype(BF16) for h in heads
        ]
        inverse = [inverse[h] - dot_nn(inverse[h], inside[h]).astype(BF16) for h in heads]
        size *= 2
    residual = [
        (eye - inverse[h].astype(F32) - dot_nn(wide(system[h]), twice(inverse[h], 0))).astype(BF16)
        for h in heads
    ]
    solve = [inverse[h].astype(F32) + dot_nn(inverse[h], residual[h]) for h in heads]

    key_pair = [twice(k, 0) for k in key]
    key_t_pair = [twice(k, 1) for k in key_t]
    value = [v_ref[:, h * DV : (h + 1) * DV] for h in heads]
    weight_row = [beta_row[h : h + 1] * enter_row[h : h + 1] * key_row[h // 2] for h in heads]
    leave_col = [
        jnp.where(leaves, jnp.exp(jnp.minimum(cum_col[h][TOK - 1 :] - cum_col[h], 0.0)), 0.0)
        * key_col[h // 2]
        for h in heads
    ]
    left = [leave_col[h] * solve[h] for h in heads]
    offset_in = [
        dot_nt(twice(value[h].T, 1), wide(left[h] * beta_row[h : h + 1])) for h in heads
    ]
    change_in = [dot_nt(key_t_pair[h // 2], wide(left[h] * weight_row[h])) for h in heads]
    offset = [dot_nn(wide(offset_in[h]), key_pair[h // 2]).astype(BF16) for h in heads]
    change = [dot_nn(wide(change_in[h]), key_pair[h // 2]).astype(BF16) for h in heads]
    at_row = iota((16, TOK), 0)
    for h in heads:
        keep = jnp.broadcast_to(enter_row[h : h + 1, TOK - 1 :], (16, TOK))
        keep_high = keep.astype(BF16)
        keep_mid, keep_low = halves(keep - keep_high.astype(F32))
        terms = jnp.where(
            at_row == 0,
            keep_high.astype(F32),
            jnp.where(
                at_row == 1,
                keep_mid.astype(F32),
                jnp.where(at_row == 2, keep_low.astype(F32), 0.0),
            ),
        ).astype(BF16)
        for s in range(2):
            maps_ref[2 * h + s, 0:64, :] = offset[h][s * 64 : (s + 1) * 64]
            maps_ref[2 * h + s, 64:192, :] = change[h]
            maps_ref[2 * h + s, 192:208, :] = terms

    mixed = []
    for h in heads:
        score_high, score_low = halves(decay[h] * cross[h // 2])
        solve_high, solve_low = halves(solve[h])
        mixed.append(
            dot_nn(
                jnp.concatenate([score_high, score_low, score_high], axis=1),
                jnp.concatenate([solve_high, solve_high, solve_low], axis=0),
            )
        )
    for h in heads:
        local_ref[:, h * DV : (h + 1) * DV] = dot_nn(
            wide(mixed[h] * beta_row[h : h + 1]), twice(value[h], 0)
        )
    for h in heads:
        enter_col = jnp.where(enters, jnp.exp(cum_col[h]), 0.0) * query_col[h // 2]
        query_ref[h] = enter_col * query_f[h // 2] - dot_nn(
            wide(mixed[h] * weight_row[h]), key_pair[h // 2]
        )


def mixer_call(lengths, queries, key_in, value_in, log_decay, beta_logit):
    steps = HV // HEADS_STEP
    return pl.pallas_call(
        mixer_kernel,
        grid=(steps,),
        in_specs=[
            pl.BlockSpec(memory_space=pltpu.SMEM),
            pl.BlockSpec((TOK, HK * DK // steps), lambda i: (0, i)),
            pl.BlockSpec((TOK, HK * DK // steps), lambda i: (0, i)),
            pl.BlockSpec((TOK, HV * DV // steps), lambda i: (0, i)),
            pl.BlockSpec((HEADS_STEP, TOK), lambda i: (i, 0)),
            pl.BlockSpec((HEADS_STEP, TOK), lambda i: (i, 0)),
        ],
        out_specs=[
            pl.BlockSpec((2 * HEADS_STEP, MAP_ROWS, DK), lambda i: (i, 0, 0)),
            pl.BlockSpec((HEADS_STEP, TOK, DK), lambda i: (i, 0, 0)),
            pl.BlockSpec((TOK, HV * DV // steps), lambda i: (0, i)),
        ],
        out_shape=[
            jax.ShapeDtypeStruct((2 * HV, MAP_ROWS, DK), BF16),
            jax.ShapeDtypeStruct((HV, TOK, DK), F32),
            jax.ShapeDtypeStruct((TOK, HV * DV), F32),
        ],
        compiler_params=params(),
        name="mixer_block",
    )(lengths, queries, key_in, value_in, log_decay, beta_logit)


def scan_kernel(maps_ref, out_ref):
    blocks = maps_ref.shape[0]
    state = jnp.zeros((64, DK), F32)
    for at in range(blocks):
        high, low = halves(state)
        out_ref[at * 64 : (at + 1) * 64, :] = high
        if at < blocks - 1:
            offset = maps_ref[at, 0:64, :].astype(F32)
            change = maps_ref[at, 64:192, :]
            keep = jnp.sum(maps_ref[at, 192:208, :].astype(F32), 0, keepdims=True)
            moved = dot_nn(jnp.concatenate([high, low], axis=0), change)
            state = keep * state - (moved[:64] + moved[64:]) + offset


def scan_call(maps):
    blocks = maps.shape[0]
    return pl.pallas_call(
        scan_kernel,
        out_shape=jax.ShapeDtypeStruct((blocks * 64, DK), BF16),
        compiler_params=params(),
        name="state_scan",
    )(maps)


def finish_kernel(
    state_ref,
    query_ref,
    local_ref,
    gate_ref,
    resid_ref,
    gain_ref,
    proj_ref,
    post_ref,
    hidden_ref,
    rows_ref,
):
    gain = gain_ref[...]
    normed = []
    for h in range(HV):
        cut = slice(h * DV, (h + 1) * DV)
        outputs = local_ref[:, cut] + dot_nt(wide(query_ref[h]), twice(state_ref[cut, :], 1))
        scale = lax.rsqrt(jnp.mean(outputs * outputs, -1, keepdims=True) + EPSILON)
        gate = gate_ref[:, cut].astype(F32)
        normed.append((outputs * scale * gain * (gate / (1.0 + jnp.exp(-gate)))).astype(BF16))
    normed = jnp.concatenate(normed, axis=1)
    total = jnp.zeros((TOK, 1), F32)
    parts = []
    for g in range(GROUPS):
        cut = slice(g * WIDTH, (g + 1) * WIDTH)
        hidden = (resid_ref[:, cut].astype(F32) + dot_nn(normed, proj_ref[:, cut])).astype(BF16)
        hidden_ref[:, cut] = hidden
        hidden = hidden.astype(F32)
        total = total + jnp.sum(hidden * hidden, -1, keepdims=True)
        parts.append(hidden)
    scale = lax.rsqrt(total / D + EPSILON)
    for g in range(GROUPS):
        cut = slice(g * WIDTH, (g + 1) * WIDTH)
        rows_ref[g * TOK : (g + 1) * TOK, :] = (parts[g] * scale * post_ref[:, cut]).astype(BF16)


def finish_call(state, query, local, gate_in, residual_in, head_gain, out_proj, post_gain):
    return pl.pallas_call(
        finish_kernel,
        out_shape=[
            jax.ShapeDtypeStruct((TOK, D), BF16),
            jax.ShapeDtypeStruct((GROUPS * TOK, WIDTH), BF16),
        ],
        compiler_params=params(),
        name="mixer_finish",
    )(state, query, local, gate_in, residual_in, head_gain, out_proj, post_gain)


def route_kernel(routes_ref, gates_ref, code_ref, code_t_ref, gate_ref):
    experts = code_ref.shape[1]
    half = experts // 2
    lane = iota((TOK, experts), 1)
    expert = jnp.where(lane < half, 2 * lane, 2 * (lane - half) + 1)
    hit = jnp.zeros((TOK, experts), F32)
    gate = jnp.zeros((TOK, experts), F32)
    for k in range(TOPK):
        match = routes_ref[:, k : k + 1] == expert
        hit = jnp.where(match, 1.0, hit)
        gate = jnp.where(match, gates_ref[:, k : k + 1], gate)
    square = (TOK, TOK)
    before = (iota(square, 0) > iota(square, 1)).astype(BF16)
    rank = dot_nn(before, hit.astype(BF16))
    code = jnp.where(hit > 0.0, rank, -1.0)
    code_ref[...] = code.astype(BF16)
    code_t_ref[0:half, :] = code[:, :half].T
    code_t_ref[half:, :] = code[:, half:].T
    high, low = halves(gate)
    gate_ref[0:TOK, :] = high
    gate_ref[TOK:, :] = low


def route_call(routes, gates, experts):
    return pl.pallas_call(
        route_kernel,
        out_shape=[
            jax.ShapeDtypeStruct((TOK, experts), BF16),
            jax.ShapeDtypeStruct((experts, TOK), F32),
            jax.ShapeDtypeStruct((2 * TOK, experts), BF16),
        ],
        compiler_params=params(),
        name="routing",
    )(routes, gates)


def dispatch_kernel(code_ref, rows_ref, out_ref):
    count = code_ref.shape[0]
    shape = (count, SPAN, TOK)
    at = iota(shape, 1)
    code = jnp.broadcast_to(code_ref[...][:, None, :], shape)
    match = code == (at % CAP).astype(F32)
    group = at // CAP
    pick = jnp.concatenate(
        [
            jnp.where(match & (group == g), 1.0, 0.0).reshape(count * SPAN, TOK).astype(BF16)
            for g in range(GROUPS)
        ],
        axis=1,
    )
    out_ref[...] = dot_nn(pick, rows_ref[...]).astype(BF16)


def dispatch_call(code_t, rows, local, devices):
    tile = 32
    steps = devices // tile
    return pl.pallas_call(
        dispatch_kernel,
        grid=(steps,),
        in_specs=[
            pl.BlockSpec((tile, TOK), lambda i: (local * steps + i, 0)),
            pl.BlockSpec((GROUPS * TOK, WIDTH), lambda i: (0, 0)),
        ],
        out_specs=pl.BlockSpec((tile * SPAN, WIDTH), lambda i: (i, 0)),
        out_shape=jax.ShapeDtypeStruct((devices * SPAN, WIDTH), BF16),
        compiler_params=params(),
        name="dispatch_rows",
    )(code_t, rows)


def expert_kernel(rows_ref, in_ref, out_ref, result_ref, x_ref, y_ref):
    count = rows_ref.shape[0] // GROUP_ROWS
    square = (GROUP_ROWS, GROUP_ROWS)
    to_at, from_at = iota(square, 0), iota(square, 1)

    def source_of(at):
        group, rest = at // PIECE, at % PIECE
        return (rest // CAP) * SPAN + group * CAP + rest % CAP

    order = (source_of(to_at) == from_at).astype(BF16)
    back = (source_of(from_at) == to_at).astype(BF16)
    for i in range(count):
        block = rows_ref[i * GROUP_ROWS : (i + 1) * GROUP_ROWS, :]
        moved = dot_nn(order, block).astype(BF16)
        for g in range(GROUPS):
            x_ref[i * PIECE : (i + 1) * PIECE, g * WIDTH : (g + 1) * WIDTH] = moved[
                g * PIECE : (g + 1) * PIECE
            ]
    x = x_ref[...]
    gate = dot_nn(x, in_ref[:, :FF])
    up = dot_nn(x, in_ref[:, FF:])
    hidden = (gate / (1.0 + jnp.exp(-gate)) * up).astype(BF16)
    y_ref[...] = dot_nn(hidden, out_ref[...]).astype(BF16)
    for i in range(count):
        block = jnp.concatenate(
            [
                y_ref[i * PIECE : (i + 1) * PIECE, g * WIDTH : (g + 1) * WIDTH]
                for g in range(GROUPS)
            ],
            axis=0,
        )
        result_ref[i * GROUP_ROWS : (i + 1) * GROUP_ROWS, :] = dot_nn(back, block).astype(BF16)


def expert_call(rows, expert_in, expert_out, local):
    total = rows.shape[0]
    steps = 2
    tile = total // steps
    tokens = tile // GROUPS
    return pl.pallas_call(
        expert_kernel,
        grid=(steps,),
        in_specs=[
            pl.BlockSpec((tile, WIDTH), lambda i: (i, 0)),
            pl.BlockSpec((None, D, 2 * FF), lambda i: (local, 0, 0)),
            pl.BlockSpec((None, FF, D), lambda i: (local, 0, 0)),
        ],
        out_specs=pl.BlockSpec((tile, WIDTH), lambda i: (i, 0)),
        out_shape=jax.ShapeDtypeStruct((total, WIDTH), BF16),
        scratch_shapes=[pltpu.VMEM((tokens, D), BF16), pltpu.VMEM((tokens, D), BF16)],
        compiler_params=params(),
        name="expert",
    )(rows, expert_in, expert_out)


def combine_kernel(code_ref, gate_ref, rows_ref, before_ref, *rest, last):
    if last:
        hidden_ref, out_ref, total_ref = rest
    else:
        out_ref, total_ref = rest
    step = pl.program_id(0)
    tile = rows_ref.shape[0]
    devices = code_ref.shape[1]
    spread_shape = (devices, tile)
    owner = (iota(spread_shape, 1) + step * tile) // SPAN
    spread = (owner == iota(spread_shape, 0)).astype(BF16)
    code = dot_nn(code_ref[...], spread)
    gate = dot_nn(gate_ref[...], spread).astype(BF16)
    at = iota((TOK, tile), 1) + step * tile
    match = code == (at % CAP).astype(F32)
    group = at // CAP % GROUPS
    zero = jnp.zeros((TOK, tile), BF16)
    weights = []
    for g in range(GROUPS):
        chosen = match & (group == g)
        weights.append(jnp.where(chosen, gate[:TOK], zero))
        weights.append(jnp.where(chosen, gate[TOK:], zero))
    part = dot_nn(jnp.concatenate(weights, axis=0), rows_ref[...])

    @pl.when(step == 0)
    def _():
        total_ref[...] = part

    @pl.when(step > 0)
    def _():
        total_ref[...] += part

    @pl.when(step == pl.num_programs(0) - 1)
    def _():
        for g in range(GROUPS):
            base = 2 * g * TOK
            mix = total_ref[base : base + TOK, :] + total_ref[base + TOK : base + 2 * TOK, :]
            cut = slice(g * WIDTH, (g + 1) * WIDTH)
            if last:
                out_ref[:, cut] = (
                    hidden_ref[:, cut].astype(F32) + (before_ref[:, cut] + mix)
                ).astype(BF16)
            else:
                out_ref[:, cut] = mix


def combine_call(code, gate, rows, local, before=None, hidden=None):
    total = rows.shape[0]
    steps = 4
    tile = total // steps
    devices = code.shape[1] // 2
    last = before is not None
    in_specs = [
        pl.BlockSpec((TOK, devices), lambda i: (0, local)),
        pl.BlockSpec((2 * TOK, devices), lambda i: (0, local)),
        pl.BlockSpec((tile, WIDTH), lambda i: (i, 0)),
    ]
    operands = [code, gate, rows]
    if last:
        in_specs += [pl.BlockSpec((TOK, D), lambda i: (0, 0))] * 2
        operands += [before, hidden]

    def body(code_ref, gate_ref, rows_ref, *rest):
        if last:
            combine_kernel(code_ref, gate_ref, rows_ref, *rest, last=True)
        else:
            combine_kernel(code_ref, gate_ref, rows_ref, None, *rest, last=False)

    return pl.pallas_call(
        body,
        grid=(steps,),
        in_specs=in_specs,
        out_specs=pl.BlockSpec((TOK, D), lambda i: (0, 0)),
        out_shape=jax.ShapeDtypeStruct((TOK, D), BF16 if last else F32),
        scratch_shapes=[pltpu.VMEM((2 * GROUPS * TOK, WIDTH), F32)],
        compiler_params=params(),
        name="combine_last" if last else "combine_first",
    )(*operands)


def exchange(rows, axes):
    return lax.all_to_all(rows, axes, split_axis=0, concat_axis=0, tiled=True)


def per_device(
    queries,
    key_in,
    value_in,
    gate_in,
    residual_in,
    log_decay,
    beta_logit,
    lengths,
    head_gain,
    out_proj,
    post_gain,
    expert_in,
    expert_out,
    routes,
    route_gates,
):
    devices = lax.axis_size("dp") * lax.axis_size("ctx")
    maps, query, local = mixer_call(
        lengths, queries[0], key_in[0], value_in[0], log_decay[0], beta_logit[0]
    )
    code, code_t, gate = route_call(routes[0], route_gates[0], 2 * devices)
    states = exchange(scan_call(exchange(maps, "ctx")), "ctx")
    hidden, rows = finish_call(
        states,
        query,
        local,
        gate_in[0],
        residual_in[0],
        head_gain[None],
        out_proj,
        post_gain[None],
    )
    both = ("dp", "ctx")

    def chunks(x):
        return x.reshape(devices, SPAN, WIDTH)

    def flat(x):
        return x.reshape(devices * SPAN, WIDTH)

    sent = [dispatch_call(code_t, rows, j, devices) for j in range(2)]
    arrived = [flat(exchange(chunks(x), both)) for x in sent]
    results = [expert_call(arrived[j], expert_in, expert_out, j) for j in range(2)]
    returned = [flat(exchange(chunks(x), both)) for x in results]
    first = combine_call(code, gate, returned[0], 0)
    return combine_call(code, gate, returned[1], 1, first, hidden)[None]


def solution(mesh):
    tokens = P("dp", "ctx", None)
    heads = P("dp", None, "ctx")
    experts = P(("dp", "ctx"), None, None)
    in_specs = (tokens,) * 5 + (heads, heads, P("dp", None), P(), P(), P())
    in_specs += (experts, experts, tokens, tokens)
    return jax.shard_map(
        per_device, mesh=mesh, in_specs=in_specs, out_specs=tokens, check_vma=False
    )
```

time: 869 us -> 281 us (0.32)
  other arithmetic: 181 us -> 0 us
  waiting for transfers between devices: 298 us -> 143 us
  blocking collectives: 168 us -> 32.7 us
  local copies, waits for them, and re-layouts: 134 us -> 13 us
  Pallas kernels: 0 us -> 64.7 us
  matrix products: 59.7 us -> 0 us
  starting transfers between devices: 6.07 us -> 26.2 us
  between operations: 15 us -> 0.15 us
    all_gather x2 -> x0, waiting for transfers between devices: 223 us -> none  [entering(): gathered = jax.tree.map(lambda a: lax.all_gather(a, axis), part)]
    another operation x7 -> x0, other arithmetic: 162 us -> none  [the longest x2 158 us: block_terms(): jax.scipy.linalg.solve_triangular(system, right_side, lower=True, unit_di...]
    all_to_all x1, blocking collectives: 168 us -> 32.7 us  [exchange(): return lax.all_to_all(rows, axes, split_axis=0, concat_axis=0, tiled=True)]
    all_to_all x1 -> x5, waiting for transfers between devices: 75.1 us -> 143 us  [exchange(): return lax.all_to_all(rows, axes, split_axis=0, concat_axis=0, tiled=True)]
    pallas_call x0 -> x10, Pallas kernels: none -> 64.7 us  [the longest x2 23.5 us: expert_call(): pl.pallas_call(expert_kernel, grid=(steps,), in_specs=[pl.BlockSpec((tile...]
    dot_general x17 -> x0, matrix products: 57.7 us -> none  [the longest x7 14.3 us: apply_map(): return jnp.einsum('hde,hef->hdf', transition, carried, precision=HIGHEST)]
    reshape x4 -> x0, local copies, waits for them, and re-layouts: 39.1 us -> none  [the longest x2 19.1 us: per_device(): outbound = outbound.reshape(device_count, local_experts, capacity, D)]
    convert_element_type x2 -> x0, local copies, waits for them, and re-layouts: 28.3 us -> none  [the longest x1 17.9 us: expert_apply(): return jnp.einsum('sjcf,jfd->sjcd', hidden_units, expert_out, preferred_e...]
  transfers between devices with their start and end apart: 3 -> 5, of which waited for: 3 -> 5; matrix products, arithmetic and copies ran while one was open for 1% -> 0% of each run, Pallas kernels for 0% -> 12%
where the time goes in v1:
time: 281 us; the launch traced here: 280 us
  waiting for transfers between devices  143 us (51%)
  Pallas kernels  64.7 us (23%)
  blocking collectives  32.7 us (12%)
  starting transfers between devices  26.2 us (9%)
  local copies, waits for them, and re-layouts  13 us (5%)
    all_to_all x5, waiting for transfers between devices, exchange(): return lax.all_to_all(rows, axes, split_axis=0, concat_axis=0, tiled=True)  143 us
    all_to_all x1, blocking collectives, exchange(): return lax.all_to_all(rows, axes, split_axis=0, concat_axis=0, tiled=True)  32.7 us
    all_to_all x5, starting transfers between devices, exchange(): return lax.all_to_all(rows, axes, split_axis=0, concat_axis=0, tiled=True)  26.2 us
    pallas_call x2, Pallas kernels, expert_call(): pl.pallas_call(expert_kernel, grid=(steps,), in_specs=[pl.BlockSpec((tile...  23.5 us
    pallas_call x2, Pallas kernels, combine_call(): pl.pallas_call(body, grid=(steps,), in_specs=in_specs, out_specs=pl.Block...  13.8 us
    unnamed x36, local copies, waits for them, and re-layouts  13 us
    pallas_call x1, Pallas kernels, mixer_call(): pl.pallas_call(mixer_kernel, grid=(steps,), in_specs=[pl.BlockSpec(memory...  9.4 us
    pallas_call x2, Pallas kernels, dispatch_call(): pl.pallas_call(dispatch_kernel, grid=(steps,), in_specs=[pl.BlockSpec((ti...  7.07 us
  transfers between devices with their start and end apart: 5, of which 5 were waited for; matrix products, arithmetic and copies ran while one was open for 0% of the time, Pallas kernels for 12%

profile of v1, /device:TPU:1, one launch (start us, length us, event | category | flops | bytes accessed | tf_op | source)
XLA Modules:
  0.0 279.5 jit_solution(11451192291882220718)
XLA Ops:
  0.0 0.0 copy-start.2
  0.0 1.0 copy-done.2
  1.0 0.0 copy-start.7
  1.0 0.9 copy-done.7
  2.0 0.0 copy-start.8
  2.0 0.9 copy-done.8
  2.9 0.0 copy-start.9
  2.9 0.7 copy-done.9
  3.6 0.0 copy-start.10
  3.6 0.7 copy-done.10
  4.3 0.0 copy-start.12
  4.3 0.7 copy-done.12
  5.0 9.4 %mixer_block.1 = (bf16[32,208,128]{2,1,0:T(8,128)(2,1)S(1)}, f32[16,128,128]{2,1,0:T(8,128)S(1)}, f32[128,2048]{1,0:T(8,128)S(1)}) custom-call(s32[1,4]{1,0:T(1,128)S(1)} %copy-done.12, bf16[128,1024]{1,0:T(8,128)(2,1)S(1)} %bitcast.29, bf16[128,1024]{1,0:T(8,128)(2,1)S(1)} %bitcast.30, bf16[128,2048]{1,0:T(8,128)(2,1)S(1)} %bitcast.24, ...), custom_call_target="tpu_custom_call" | custom-call | tf_op jit(solution)/shard_map/mixer_block/pallas_call | solution.py:217
  14.4 0.0 copy-start.15
  14.4 0.0 copy-start.16
  14.4 0.0 copy-start.11
  14.4 0.0 copy-start.13
  14.5 32.7 %all_to_all.36.maps_ref = bf16[32,208,128]{2,1,0:T(8,128)(2,1)S(1)} all-to-all(bf16[32,208,128]{2,1,0:T(8,128)(2,1)S(1)} %get-tuple-element.16), channel_id=1, replica_groups=mesh['dp'=4,'ctx'=32] {'ctx'}, dimensions={0} | all-to-all | bytes 3407872 | tf_op jit(solution)/shard_map/all_to_all | solution.py:521
  47.1 4.7 %state_scan.1 = bf16[2048,128]{1,0:T(8,128)(2,1)} custom-call(bf16[32,208,128]{2,1,0:T(8,128)(2,1)S(1)} %all_to_all.36.maps_ref), custom_call_target="tpu_custom_call" | custom-call | tf_op jit(solution)/shard_map/state_scan/pallas_call | solution.py:259
  51.9 4.1 %all-to-all-start.1 = ((bf16[32,64,128]{2,1,0:T(8,128)(2,1)}), bf16[32,64,128]{2,1,0:T(8,128)(2,1)S(1)}, u32[]{:S(2)}, u32[]{:S(2)}) async-start(bf16[32,64,128]{2,1,0:T(8,128)(2,1)} %bitcast.7), calls=%async_computation.1 | async-start | bytes 1048576 | tf_op jit(solution)/shard_map/all_to_all | solution.py:521
  56.0 0.0 copy-done.15
  56.0 0.1 copy.16
  56.1 0.0 copy-done.16
  56.1 0.1 copy.17
  56.2 0.7 routing.1
  56.9 10.8 %all-to-all-done.1 = bf16[32,64,128]{2,1,0:T(8,128)(2,1)S(1)} async-done(((bf16[32,64,128]{2,1,0:T(8,128)(2,1)}), bf16[32,64,128]{2,1,0:T(8,128)(2,1)S(1)}, u32[]{:S(2)}, u32[]{:S(2)}) %all-to-all-start.1) | async-done | bytes 524320 | tf_op jit(solution)/shard_map/all_to_all | solution.py:521
  67.6 0.0 copy-done.11
  67.6 0.0 copy-done.13
  67.6 0.0 copy-start.5
  67.6 1.0 copy-done.5
  68.7 0.0 copy-start.6
  68.7 1.0 copy-done.6
  69.7 5.6 %mixer_finish.1 = (bf16[128,2048]{1,0:T(8,128)(2,1)S(1)}, bf16[512,512]{1,0:T(8,128)(2,1)S(1)}) custom-call(bf16[2048,128]{1,0:T(8,128)(2,1)S(1)} %bitcast.23, f32[16,128,128]{2,1,0:T(8,128)S(1)} %get-tuple-element.17.query_ref, f32[128,2048]{1,0:T(8,128)S(1)} %get-tuple-element.18.local_ref, bf16[128,2048]{1,0:T(8,128)(2,1)S(1)} %bitcast.25, ...), custom_call_target="tpu_custom_call" | custom-call | tf_op jit(solution)/shard_map/mixer_finish/pallas_call | solution.py:304
  75.3 0.0 copy-start.3
  75.3 0.8 copy-done.3
  76.1 3.5 %dispatch_rows.3 = bf16[3072,512]{1,0:T(8,128)(2,1)} custom-call(f32[256,128]{1,0:T(8,128)S(1)} %get-tuple-element.15.code_ref, bf16[512,512]{1,0:T(8,128)(2,1)S(1)} %get-tuple-element.19.rows_ref), custom_call_target="tpu_custom_call" | custom-call | tf_op jit(solution)/shard_map/dispatch_rows/pallas_call | solution.py:371
  79.6 7.2 %all-to-all-start.4 = ((bf16[128,24,512]{2,1,0:T(8,128)(2,1)}), bf16[128,24,512]{2,1,0:T(8,128)(2,1)}, u32[]{:S(2)}, u32[]{:S(2)}) async-start(bf16[128,24,512]{2,1,0:T(8,128)(2,1)} %bitcast.17), calls=%async_computation.4 | async-start | bytes 6291456 | tf_op jit(solution)/shard_map/all_to_all | solution.py:521
  86.8 3.5 %dispatch_rows.2 = bf16[3072,512]{1,0:T(8,128)(2,1)} custom-call(f32[256,128]{1,0:T(8,128)S(1)} %get-tuple-element.15.code_ref, bf16[512,512]{1,0:T(8,128)(2,1)S(1)} %get-tuple-element.19.rows_ref), custom_call_target="tpu_custom_call" | custom-call | tf_op jit(solution)/shard_map/dispatch_rows/pallas_call | solution.py:371
  90.4 37.7 %all-to-all-done.4 = bf16[128,24,512]{2,1,0:T(8,128)(2,1)} async-done(((bf16[128,24,512]{2,1,0:T(8,128)(2,1)}), bf16[128,24,512]{2,1,0:T(8,128)(2,1)}, u32[]{:S(2)}, u32[]{:S(2)}) %all-to-all-start.4) | async-done | bytes 3145760 | tf_op jit(solution)/shard_map/all_to_all | solution.py:521
  128.1 4.6 %all-to-all-start.2 = ((bf16[128,24,512]{2,1,0:T(8,128)(2,1)}), bf16[128,24,512]{2,1,0:T(8,128)(2,1)S(1)}, u32[]{:S(2)}, u32[]{:S(2)}) async-start(bf16[128,24,512]{2,1,0:T(8,128)(2,1)} %bitcast.13), calls=%async_computation.2 | async-start | bytes 6291456 | tf_op jit(solution)/shard_map/all_to_all | solution.py:521
  132.7 11.7 %expert.3 = bf16[3072,512]{1,0:T(8,128)(2,1)} custom-call(bf16[3072,512]{1,0:T(8,128)(2,1)} %bitcast.18.rows_ref, bf16[2,2048,1024]{2,1,0:T(8,128)(2,1)} %in_ref.3, bf16[2,512,2048]{2,1,0:T(8,128)(2,1)} %out_ref.3), custom_call_target="tpu_custom_call" | custom-call | tf_op jit(solution)/shard_map/expert/pallas_call | solution.py:424
  144.4 29.9 %all-to-all-done.2 = bf16[128,24,512]{2,1,0:T(8,128)(2,1)S(1)} async-done(((bf16[128,24,512]{2,1,0:T(8,128)(2,1)}), bf16[128,24,512]{2,1,0:T(8,128)(2,1)S(1)}, u32[]{:S(2)}, u32[]{:S(2)}) %all-to-all-start.2) | async-done | bytes 3145760 | tf_op jit(solution)/shard_map/all_to_all | solution.py:521
  174.4 0.0 copy-start.14
  174.4 1.7 copy-done.14
  176.1 4.6 %all-to-all-start.5 = ((bf16[128,24,512]{2,1,0:T(8,128)(2,1)}), bf16[128,24,512]{2,1,0:T(8,128)(2,1)S(1)}, u32[]{:S(2)}, u32[]{:S(2)}) async-start(bf16[128,24,512]{2,1,0:T(8,128)(2,1)} %bitcast.19), calls=%async_computation.5 | async-start | bytes 6291456 | tf_op jit(solution)/shard_map/all_to_all | solution.py:521
  180.7 11.8 %expert.2 = bf16[3072,512]{1,0:T(8,128)(2,1)} custom-call(bf16[3072,512]{1,0:T(8,128)(2,1)} %bitcast.35, bf16[2,2048,1024]{2,1,0:T(8,128)(2,1)} %in_ref.3, bf16[2,512,2048]{2,1,0:T(8,128)(2,1)} %out_ref.3), custom_call_target="tpu_custom_call" | custom-call | tf_op jit(solution)/shard_map/expert/pallas_call | solution.py:424
  192.5 29.9 %all-to-all-done.5 = bf16[128,24,512]{2,1,0:T(8,128)(2,1)S(1)} async-done(((bf16[128,24,512]{2,1,0:T(8,128)(2,1)}), bf16[128,24,512]{2,1,0:T(8,128)(2,1)S(1)}, u32[]{:S(2)}, u32[]{:S(2)}) %all-to-all-start.5) | async-done | bytes 3145760 | tf_op jit(solution)/shard_map/all_to_all | solution.py:521
  222.4 5.6 %all-to-all-start.3 = ((bf16[128,24,512]{2,1,0:T(8,128)(2,1)}), bf16[128,24,512]{2,1,0:T(8,128)(2,1)}, u32[]{:S(2)}, u32[]{:S(2)}) async-start(bf16[128,24,512]{2,1,0:T(8,128)(2,1)} %bitcast.15), calls=%async_computation.3 | async-start | bytes 6291456 | tf_op jit(solution)/shard_map/all_to_all | solution.py:521
  228.0 5.9 %combine_first.1.rest_0_ = f32[128,2048]{1,0:T(8,128)S(1)} custom-call(bf16[128,256]{1,0:T(8,128)(2,1)S(1)} %get-tuple-element.13.code_ref, bf16[256,256]{1,0:T(8,128)(2,1)S(1)} %get-tuple-element.14.gate_ref, bf16[3072,512]{1,0:T(8,128)(2,1)S(1)} %bitcast.22), custom_call_target="tpu_custom_call" | custom-call | tf_op jit(solution)/shard_map/combine_first/pallas_call | solution.py:508
  233.9 0.0 copy-start
  233.9 0.9 copy-done
  234.9 34.5 %all-to-all-done.3 = bf16[128,24,512]{2,1,0:T(8,128)(2,1)} async-done(((bf16[128,24,512]{2,1,0:T(8,128)(2,1)}), bf16[128,24,512]{2,1,0:T(8,128)(2,1)}, u32[]{:S(2)}, u32[]{:S(2)}) %all-to-all-start.3) | async-done | bytes 3145760 | tf_op jit(solution)/shard_map/all_to_all | solution.py:521
  269.4 0.0 copy-start.1
  269.4 1.2 copy-done.1
  270.6 0.0 copy-start.4
  270.6 1.0 copy-done.4
  271.6 7.9 %combine_last.1 = bf16[128,2048]{1,0:T(8,128)(2,1)} custom-call(bf16[128,256]{1,0:T(8,128)(2,1)S(1)} %get-tuple-element.13.code_ref, bf16[256,256]{1,0:T(8,128)(2,1)S(1)} %get-tuple-element.14.gate_ref, bf16[3072,512]{1,0:T(8,128)(2,1)} %bitcast.16.rows_ref, f32[128,2048]{1,0:T(8,128)S(1)} %copy-done.1, bf16[128,2048]{1,0:T(8,128)(2,1)S(1)} %copy-done.4), custom_call_target="tpu_custom_call" | custom-call | tf_op jit(solution)/shard_map/combine_last/pallas_call | solution.py:508
Async XLA Ops:
  0.0 1.0 copy-start.2
  1.0 0.9 copy-start.7
  2.0 0.9 copy-start.8
  2.9 0.7 copy-start.9
  3.6 0.7 copy-start.10
  4.3 0.7 copy-start.12
  14.4 41.6 %copy-start.15 = (s32[1,128,10]{1,0,2:T(1,128)S(1)}, s32[1,128,10]{1,0,2:T(1,128)}, u32[]{:S(2)}) copy-start(s32[1,128,10]{1,0,2:T(1,128)} %param.28) | copy-start | bytes 15364
  14.4 41.7 %copy-start.16 = (f32[1,128,10]{1,0,2:T(1,128)S(1)}, f32[1,128,10]{1,0,2:T(1,128)}, u32[]{:S(2)}) copy-start(f32[1,128,10]{1,0,2:T(1,128)} %param.29) | copy-start | bytes 15364
  14.4 53.2 %copy-start.11 = (f32[2048]{0:T(1024)S(1)}, f32[2048]{0:T(1024)}, u32[]{:S(2)}) copy-start(f32[2048]{0:T(1024)} %param.25) | copy-start | bytes 24580
  14.4 53.2 %copy-start.13 = (f32[128]{0:T(128)S(1)}, f32[128]{0:T(128)}, u32[]{:S(2)}) copy-start(f32[128]{0:T(128)} %param.23) | copy-start | bytes 1540
  51.9 15.8 %all-to-all-start.1 = ((bf16[32,64,128]{2,1,0:T(8,128)(2,1)}), bf16[32,64,128]{2,1,0:T(8,128)(2,1)S(1)}, u32[]{:S(2)}, u32[]{:S(2)}) async-start(bf16[32,64,128]{2,1,0:T(8,128)(2,1)} %bitcast.7), calls=%async_computation.1 | async-start | bytes 1048576 | tf_op jit(solution)/shard_map/all_to_all | solution.py:521
  67.6 1.0 copy-start.5
  68.7 1.0 copy-start.6
  75.3 0.8 copy-start.3
  79.6 48.4 %all-to-all-start.4 = ((bf16[128,24,512]{2,1,0:T(8,128)(2,1)}), bf16[128,24,512]{2,1,0:T(8,128)(2,1)}, u32[]{:S(2)}, u32[]{:S(2)}) async-start(bf16[128,24,512]{2,1,0:T(8,128)(2,1)} %bitcast.17), calls=%async_computation.4 | async-start | bytes 6291456 | tf_op jit(solution)/shard_map/all_to_all | solution.py:521
  128.1 46.3 %all-to-all-start.2 = ((bf16[128,24,512]{2,1,0:T(8,128)(2,1)}), bf16[128,24,512]{2,1,0:T(8,128)(2,1)S(1)}, u32[]{:S(2)}, u32[]{:S(2)}) async-start(bf16[128,24,512]{2,1,0:T(8,128)(2,1)} %bitcast.13), calls=%async_computation.2 | async-start | bytes 6291456 | tf_op jit(solution)/shard_map/all_to_all | solution.py:521
  174.4 1.7 copy-start.14
  176.1 46.3 %all-to-all-start.5 = ((bf16[128,24,512]{2,1,0:T(8,128)(2,1)}), bf16[128,24,512]{2,1,0:T(8,128)(2,1)S(1)}, u32[]{:S(2)}, u32[]{:S(2)}) async-start(bf16[128,24,512]{2,1,0:T(8,128)(2,1)} %bitcast.19), calls=%async_computation.5 | async-start | bytes 6291456 | tf_op jit(solution)/shard_map/all_to_all | solution.py:521
  222.4 47.0 %all-to-all-start.3 = ((bf16[128,24,512]{2,1,0:T(8,128)(2,1)}), bf16[128,24,512]{2,1,0:T(8,128)(2,1)}, u32[]{:S(2)}, u32[]{:S(2)}) async-start(bf16[128,24,512]{2,1,0:T(8,128)(2,1)} %bitcast.15), calls=%async_computation.3 | async-start | bytes 6291456 | tf_op jit(solution)/shard_map/all_to_all | solution.py:521
  233.9 1.0 copy-start
  269.4 1.2 copy-start.1
  270.6 1.0 copy-start.4

commit v2 on v1

v2 whole, which is shorter than its diff:
```python
import jax
import jax.numpy as jnp
from jax import lax
from jax.experimental import pallas as pl
from jax.experimental.pallas import tpu as pltpu
from jax.sharding import PartitionSpec as P

D = 2048
DK = 128
DV = 128
FF = 512
TOPK = 10
HK = 8
HV = 16
TOK = 128
CAP = 6
GROUPS = 4
WIDTH = D // GROUPS
SPAN = GROUPS * CAP
EPSILON = 1e-06

F32 = jnp.float32
BF16 = jnp.bfloat16
HEADS_STEP = 8
MAP_ROWS = 64 + 128 + 16
SRC_GROUP = 4
GROUP_ROWS = SRC_GROUP * SPAN
PIECE = SRC_GROUP * CAP
DISPATCH_STEPS = 8
MIB = 1 << 20


def dot_nn(a, b):
    return lax.dot_general(a, b, (((1,), (0,)), ((), ())), preferred_element_type=F32)


def dot_nt(a, b):
    return lax.dot_general(a, b, (((1,), (1,)), ((), ())), preferred_element_type=F32)


def halves(x):
    high = x.astype(BF16)
    return high, (x - high.astype(F32)).astype(BF16)


def wide(x):
    high, low = halves(x)
    return jnp.concatenate([high, low], axis=1)


def twice(x, axis):
    return jnp.concatenate([x, x], axis=axis)


def iota(shape, axis):
    return lax.broadcasted_iota(jnp.int32, shape, axis)


def params(limit=60 * MIB):
    return pltpu.CompilerParams(vmem_limit_bytes=limit)


def block_frame(len_ref, k_ref, decay_ref, beta_ref):
    first = lax.axis_index("ctx") * TOK
    start1 = len_ref[0, 0]
    start2 = start1 + len_ref[0, 1]
    start3 = start2 + len_ref[0, 2]

    def segment(at):
        return (
            (at >= 0).astype(jnp.int32)
            + (at >= start1).astype(jnp.int32)
            + (at >= start2).astype(jnp.int32)
            + (at >= start3).astype(jnp.int32)
        )

    square = (TOK, TOK)
    rows, cols = iota(square, 0), iota(square, 1)
    seg_before, seg_last = segment(first - 1), segment(first + TOK - 1)
    lower = (segment(first + rows) == segment(first + cols)) & (rows >= cols)
    cum_row = lax.dot_general(
        decay_ref[...],
        (rows <= cols).astype(F32),
        (((1,), (0,)), ((), ())),
        precision=lax.Precision.HIGHEST,
        preferred_element_type=F32,
    )
    beta_row = 1.0 / (1.0 + jnp.exp(-beta_ref[...]))
    columns = jnp.concatenate(
        [cum_row, beta_row, jnp.zeros((TOK - 2 * HEADS_STEP, TOK), F32)], axis=0
    ).T
    row8 = iota((HEADS_STEP, TOK), 1)
    enter_row = jnp.where(segment(first + row8) == seg_before, jnp.exp(cum_row), 0.0)
    at = first + iota((TOK, 1), 0)
    enters, leaves = segment(at) == seg_before, segment(at) == seg_last
    cum_col = [columns[:, h : h + 1] for h in range(HEADS_STEP)]
    beta_col = [columns[:, HEADS_STEP + h : HEADS_STEP + h + 1] for h in range(HEADS_STEP)]
    key = [k_ref[:, i * DK : (i + 1) * DK] for i in range(HEADS_STEP // 2)]
    inner = [dot_nt(k, k) for k in key]
    squares = [jnp.where(rows == cols, x, 0.0) for x in inner]
    key_row = [lax.rsqrt(jnp.sum(x, 0, keepdims=True) + EPSILON) for x in squares]
    key_col = [lax.rsqrt(jnp.sum(x, 1, keepdims=True) + EPSILON) for x in squares]
    decay = [
        jnp.where(
            lower, jnp.exp(jnp.minimum(cum_col[h] - cum_row[h : h + 1], 0.0)), 0.0
        )
        for h in range(HEADS_STEP)
    ]
    rows_of = (beta_row, enter_row, key_row)
    columns_of = (cum_col, beta_col, key_col, enters, leaves)
    return rows, cols, key, inner, decay, rows_of, columns_of


def maps_kernel(len_ref, k_ref, v_ref, decay_ref, beta_ref, maps_ref, solve_ref):
    rows, cols, key, inner, decay, rows_of, columns_of = block_frame(
        len_ref, k_ref, decay_ref, beta_ref
    )
    beta_row, enter_row, key_row = rows_of
    cum_col, beta_col, key_col, enters, leaves = columns_of
    square = (TOK, TOK)
    heads = range(HEADS_STEP)
    strict = rows > cols
    eye = (rows == cols).astype(F32)
    inner = [x * r for x, r in zip(inner, key_row)]
    system = [
        jnp.where(strict, (beta_col[h] * key_col[h // 2]) * decay[h] * inner[h // 2], 0.0)
        for h in heads
    ]
    system_bf = [x.astype(BF16) for x in system]
    zero_bf = jnp.zeros(square, BF16)
    inverse = [eye.astype(BF16)] * HEADS_STEP
    size = 1
    while size < TOK:
        mask = (rows // (2 * size) == cols // (2 * size)) & (rows // size != cols // size)
        inside = [jnp.where(mask, x, zero_bf) for x in system_bf]
        if size > 1:
            inside = [dot_nn(x, y).astype(BF16) for x, y in zip(inside, inverse)]
            inside = [dot_nn(y, x).astype(BF16) for x, y in zip(inside, inverse)]
        inverse = [y - x for x, y in zip(inside, inverse)]
        size *= 2
    residual = [
        (eye - inverse[h].astype(F32) - dot_nn(wide(system[h]), twice(inverse[h], 0))).astype(BF16)
        for h in heads
    ]
    solve = [inverse[h].astype(F32) + dot_nn(inverse[h], residual[h]) for h in heads]
    for h in heads:
        solve_ref[h] = solve[h]

    key_pair = [twice(k, 0) for k in key]
    key_t_pair = [twice(k.T, 1) for k in key]
    value_t = [v_ref[:, h * DV : (h + 1) * DV].T for h in heads]
    weight_row = [beta_row[h : h + 1] * enter_row[h : h + 1] * key_row[h // 2] for h in heads]
    leave_col = [
        jnp.where(leaves, jnp.exp(jnp.minimum(cum_col[h][TOK - 1 :] - cum_col[h], 0.0)), 0.0)
        * key_col[h // 2]
        for h in heads
    ]
    left = [leave_col[h] * solve[h] for h in heads]
    offset_in = [dot_nt(twice(value_t[h], 1), wide(left[h] * beta_row[h : h + 1])) for h in heads]
    change_in = [dot_nt(key_t_pair[h // 2], wide(left[h] * weight_row[h])) for h in heads]
    offset = [dot_nn(wide(offset_in[h]), key_pair[h // 2]).astype(BF16) for h in heads]
    change = [dot_nn(wide(change_in[h]), key_pair[h // 2]).astype(BF16) for h in heads]
    at_row = iota((16, TOK), 0)
    for h in heads:
        keep = jnp.broadcast_to(enter_row[h : h + 1, TOK - 1 :], (16, TOK))
        keep_high = keep.astype(BF16)
        keep_mid, keep_low = halves(keep - keep_high.astype(F32))
        terms = jnp.where(
            at_row == 0,
            keep_high.astype(F32),
            jnp.where(
                at_row == 1,
                keep_mid.astype(F32),
                jnp.where(at_row == 2, keep_low.astype(F32), 0.0),
            ),
        ).astype(BF16)
        for s in range(2):
            maps_ref[2 * h + s, 0:64, :] = offset[h][s * 64 : (s + 1) * 64]
            maps_ref[2 * h + s, 64:192, :] = change[h]
            maps_ref[2 * h + s, 192:208, :] = terms


def reads_kernel(
    len_ref, q_ref, k_ref, v_ref, decay_ref, beta_ref, solve_ref, query_ref, local_ref
):
    rows, cols, key, inner, decay, rows_of, columns_of = block_frame(
        len_ref, k_ref, decay_ref, beta_ref
    )
    beta_row, enter_row, key_row = rows_of
    cum_col, beta_col, key_col, enters, leaves = columns_of
    heads = range(HEADS_STEP)
    query = [q_ref[:, i * DK : (i + 1) * DK] for i in range(HEADS_STEP // 2)]
    query_f = [q.astype(F32) for q in query]
    query_col = [
        lax.rsqrt(jnp.sum(q * q, 1, keepdims=True) + EPSILON) * (DK**-0.5) for q in query_f
    ]
    cross = [dot_nt(q, k) * r * c for q, k, r, c in zip(query, key, key_row, query_col)]
    key_pair = [twice(k, 0) for k in key]
    value = [v_ref[:, h * DV : (h + 1) * DV] for h in heads]
    weight_row = [beta_row[h : h + 1] * enter_row[h : h + 1] * key_row[h // 2] for h in heads]
    mixed = []
    for h in heads:
        score_high, score_low = halves(decay[h] * cross[h // 2])
        solve_high, solve_low = halves(solve_ref[h])
        mixed.append(
            dot_nn(
                jnp.concatenate([score_high, score_low, score_high], axis=1),
                jnp.concatenate([solve_high, solve_high, solve_low], axis=0),
            )
        )
    for h in heads:
        local_ref[:, h * DV : (h + 1) * DV] = dot_nn(
            wide(mixed[h] * beta_row[h : h + 1]), twice(value[h], 0)
        )
    for h in heads:
        enter_col = jnp.where(enters, jnp.exp(cum_col[h]), 0.0) * query_col[h // 2]
        query_ref[h] = enter_col * query_f[h // 2] - dot_nn(
            wide(mixed[h] * weight_row[h]), key_pair[h // 2]
        )


STEPS = HV // HEADS_STEP
LENGTHS = pl.BlockSpec(memory_space=pltpu.SMEM)
KEY_BLOCK = pl.BlockSpec((TOK, HK * DK // STEPS), lambda i: (0, i))
VALUE_BLOCK = pl.BlockSpec((TOK, HV * DV // STEPS), lambda i: (0, i))
HEAD_BLOCK = pl.BlockSpec((HEADS_STEP, TOK), lambda i: (i, 0))
SQUARE_BLOCK = pl.BlockSpec((HEADS_STEP, TOK, TOK), lambda i: (i, 0, 0))


def maps_call(lengths, key_in, value_in, log_decay, beta_logit):
    return pl.pallas_call(
        maps_kernel,
        grid=(STEPS,),
        in_specs=[LENGTHS, KEY_BLOCK, VALUE_BLOCK, HEAD_BLOCK, HEAD_BLOCK],
        out_specs=[
            pl.BlockSpec((2 * HEADS_STEP, MAP_ROWS, DK), lambda i: (i, 0, 0)),
            SQUARE_BLOCK,
        ],
        out_shape=[
            jax.ShapeDtypeStruct((2 * HV, MAP_ROWS, DK), BF16),
            jax.ShapeDtypeStruct((HV, TOK, TOK), F32),
        ],
        compiler_params=params(),
        name="block_maps",
    )(lengths, key_in, value_in, log_decay, beta_logit)


def reads_call(lengths, queries, key_in, value_in, log_decay, beta_logit, solve):
    return pl.pallas_call(
        reads_kernel,
        grid=(STEPS,),
        in_specs=[
            LENGTHS,
            KEY_BLOCK,
            KEY_BLOCK,
            VALUE_BLOCK,
            HEAD_BLOCK,
            HEAD_BLOCK,
            SQUARE_BLOCK,
        ],
        out_specs=[SQUARE_BLOCK, VALUE_BLOCK],
        out_shape=[
            jax.ShapeDtypeStruct((HV, TOK, DK), F32),
            jax.ShapeDtypeStruct((TOK, HV * DV), F32),
        ],
        compiler_params=params(),
        name="block_reads",
    )(lengths, queries, key_in, value_in, log_decay, beta_logit, solve)


def scan_kernel(maps_ref, out_ref):
    blocks = maps_ref.shape[0]
    state = jnp.zeros((64, DK), F32)
    for at in range(blocks):
        high, low = halves(state)
        out_ref[at * 64 : (at + 1) * 64, :] = high
        if at < blocks - 1:
            offset = maps_ref[at, 0:64, :].astype(F32)
            change = maps_ref[at, 64:192, :]
            keep = jnp.sum(maps_ref[at, 192:208, :].astype(F32), 0, keepdims=True)
            moved = dot_nn(jnp.concatenate([high, low], axis=0), change)
            state = keep * state - (moved[:64] + moved[64:]) + offset


def scan_call(maps):
    blocks = maps.shape[0]
    return pl.pallas_call(
        scan_kernel,
        out_shape=jax.ShapeDtypeStruct((blocks * 64, DK), BF16),
        compiler_params=params(),
        name="state_scan",
    )(maps)


def finish_kernel(
    gain_ref,
    post_ref,
    code_ref,
    state_hbm,
    query_hbm,
    local_hbm,
    gate_hbm,
    resid_hbm,
    proj_hbm,
    hidden_hbm,
    out_hbm,
    state_ref,
    query_ref,
    local_ref,
    gate_ref,
    resid_ref,
    weight_ref,
    hidden_ref,
    rows_ref,
    out_ref,
    sems,
    weight_sems,
    hidden_sem,
    out_sems,
):
    loads = [
        pltpu.make_async_copy(source, target, sems.at[i])
        for i, (source, target) in enumerate(
            [
                (state_hbm, state_ref),
                (query_hbm, query_ref),
                (local_hbm, local_ref),
                (gate_hbm, gate_ref),
                (resid_hbm, resid_ref),
            ]
        )
    ]
    quarters = []
    for g in range(GROUPS):
        at = (slice(None), pl.ds(g * WIDTH, WIDTH))
        quarters.append(
            pltpu.make_async_copy(proj_hbm.at[at], weight_ref.at[at], weight_sems.at[g])
        )
    for load in loads:
        load.start()
    quarters[0].start()
    for load in loads:
        load.wait()
    quarters[1].start()
    gain = gain_ref[...]
    normed = []
    for h in range(HV):
        cut = slice(h * DV, (h + 1) * DV)
        outputs = local_ref[:, cut] + dot_nt(wide(query_ref[h]), twice(state_ref[cut, :], 1))
        scale = lax.rsqrt(jnp.mean(outputs * outputs, -1, keepdims=True) + EPSILON)
        gate = gate_ref[:, cut].astype(F32)
        normed.append((outputs * scale * gain * (gate / (1.0 + jnp.exp(-gate)))).astype(BF16))
    normed = jnp.concatenate(normed, axis=1)
    total = jnp.zeros((TOK, 1), F32)
    parts = []
    for g in range(GROUPS):
        cut = slice(g * WIDTH, (g + 1) * WIDTH)
        quarters[g].wait()
        if g + 2 < GROUPS:
            quarters[g + 2].start()
        mixed = dot_nn(normed, weight_ref[:, cut])
        hidden = (resid_ref[:, cut].astype(F32) + mixed).astype(BF16)
        hidden_ref[:, cut] = hidden
        hidden = hidden.astype(F32)
        total = total + jnp.sum(hidden * hidden, -1, keepdims=True)
        parts.append(hidden)
    keep = pltpu.make_async_copy(hidden_ref, hidden_hbm, hidden_sem)
    keep.start()
    scale = lax.rsqrt(total / D + EPSILON)
    for g in range(GROUPS):
        cut = slice(g * WIDTH, (g + 1) * WIDTH)
        rows_ref[g * TOK : (g + 1) * TOK, :] = (parts[g] * scale * post_ref[:, cut]).astype(BF16)

    count = code_ref.shape[0] // DISPATCH_STEPS
    stores = [keep]
    for step in range(DISPATCH_STEPS):
        code = code_ref[step * count : (step + 1) * count, :][:, None, :]
        tiles = []
        for part in range(SPAN // 8):
            at = iota((1, 8, TOK), 1) + 8 * part
            slot, group = at % CAP, at // CAP
            pick = [
                jnp.where(code == jnp.where(group == g, slot, TOK).astype(F32), 1.0, 0.0)
                .reshape(count * 8, TOK)
                .astype(BF16)
                for g in (part, part + 1)
            ]
            source = rows_ref[part * TOK : (part + 2) * TOK, :]
            tiles.append(dot_nn(jnp.concatenate(pick, axis=1), source).reshape(count, 1, 8, WIDTH))
        at = pl.ds(step * count * SPAN, count * SPAN)
        out_ref[at, :] = jnp.concatenate(tiles, axis=1).reshape(count * SPAN, WIDTH).astype(BF16)
        stores.append(pltpu.make_async_copy(out_ref.at[at], out_hbm.at[at], out_sems.at[step]))
        stores[-1].start()
    for store in stores:
        store.wait()


def finish_call(state, query, local, gate_in, residual_in, head_gain, post_gain, code_t, out_proj):
    experts = code_t.shape[0]
    large = [state, query, local, gate_in, residual_in]
    hidden = jax.ShapeDtypeStruct((TOK, D), BF16)
    sent = jax.ShapeDtypeStruct((experts * SPAN, WIDTH), BF16)
    rows = jax.ShapeDtypeStruct((GROUPS * TOK, WIDTH), BF16)
    return pl.pallas_call(
        finish_kernel,
        in_specs=[pl.BlockSpec(memory_space=pltpu.VMEM)] * 3
        + [pl.BlockSpec(memory_space=pl.ANY)] * 6,
        out_specs=[pl.BlockSpec(memory_space=pl.ANY)] * 2,
        out_shape=[hidden, sent],
        scratch_shapes=[
            pltpu.VMEM(x.shape, x.dtype) for x in large + [out_proj, hidden, rows, sent]
        ]
        + [
            pltpu.SemaphoreType.DMA((len(large),)),
            pltpu.SemaphoreType.DMA((GROUPS,)),
            pltpu.SemaphoreType.DMA,
            pltpu.SemaphoreType.DMA((DISPATCH_STEPS,)),
        ],
        compiler_params=params(),
        name="mixer_finish",
    )(head_gain, post_gain, code_t, *large, out_proj)


def route_kernel(routes_ref, gates_ref, code_ref, code_t_ref):
    experts = code_t_ref.shape[0]
    expert = iota((TOK, experts), 1)
    hit = jnp.zeros((TOK, experts), F32)
    gate = jnp.zeros((TOK, experts), F32)
    for k in range(TOPK):
        match = routes_ref[:, k : k + 1] == expert
        hit = jnp.where(match, 1.0, hit)
        gate = jnp.where(match, gates_ref[:, k : k + 1], gate)
    square = (TOK, TOK)
    before = (iota(square, 0) > iota(square, 1)).astype(BF16)
    rank = dot_nn(before, hit.astype(BF16))
    code = jnp.where(hit > 0.0, rank, -1.0)
    code_ref[0:TOK, :] = code.astype(BF16)
    code_ref[TOK:, :] = gate.astype(BF16)
    for at in range(0, experts, TOK):
        code_t_ref[at : at + TOK, :] = code[:, at : at + TOK].T


def route_call(routes, gates, experts):
    return pl.pallas_call(
        route_kernel,
        out_shape=[
            jax.ShapeDtypeStruct((2 * TOK, experts), BF16),
            jax.ShapeDtypeStruct((experts, TOK), F32),
        ],
        compiler_params=params(),
        name="routing",
    )(routes, gates)


def expert_kernel(
    rows_hbm,
    in_hbm,
    out_hbm,
    result_hbm,
    rows_ref,
    result_ref,
    x_ref,
    y_ref,
    in_vmem,
    out_vmem,
    row_sem,
    in_sem,
    out_sem,
    result_sem,
):
    local = in_vmem.shape[0]
    total = rows_ref.shape[0]
    half = total // 2
    halves_in = []
    for part in range(2):
        at = pl.ds(part * half, half)
        halves_in.append(
            pltpu.make_async_copy(rows_hbm.at[at], rows_ref.at[at], row_sem.at[part])
        )
    loads = []
    for j in range(local):
        loads.append(
            (
                pltpu.make_async_copy(in_hbm.at[j], in_vmem.at[j], in_sem.at[j]),
                pltpu.make_async_copy(out_hbm.at[j], out_vmem.at[j], out_sem.at[j]),
            )
        )
    halves_in[0].start()
    for first, second in loads:
        first.start()
        second.start()
    halves_in[1].start()

    block_rows = local * GROUP_ROWS
    count = half // block_rows
    square = (block_rows, block_rows)
    to_at, from_at = iota(square, 0), iota(square, 1)

    def source_of(at):
        piece, rest = at // PIECE, at % PIECE
        return (rest // CAP) * (local * SPAN) + piece * CAP + rest % CAP

    order = (source_of(to_at) == from_at).astype(BF16)
    back = (source_of(from_at) == to_at).astype(BF16)
    stores = []
    for part in range(2):
        base = part * half
        halves_in[part].wait()
        for i in range(0, count, 2):
            moved = [
                dot_nn(order, rows_ref[base + k * block_rows : base + (k + 1) * block_rows, :])
                for k in (i, i + 1)
            ]
            for j in range(local):
                for g in range(GROUPS):
                    cut = slice((j * GROUPS + g) * PIECE, (j * GROUPS + g + 1) * PIECE)
                    x_ref[j, i * PIECE : (i + 2) * PIECE, g * WIDTH : (g + 1) * WIDTH] = (
                        jnp.concatenate([m[cut] for m in moved], axis=0).astype(BF16)
                    )
        for j in range(local):
            x = x_ref[j]
            if part == 0:
                loads[j][0].wait()
            gate = dot_nn(x, in_vmem[j, :, :FF])
            up = dot_nn(x, in_vmem[j, :, FF:])
            hidden = (gate / (1.0 + jnp.exp(-gate)) * up).astype(BF16)
            if part == 0:
                loads[j][1].wait()
            y_ref[j] = dot_nn(hidden, out_vmem[j])
        for i in range(count):
            block = jnp.concatenate(
                [
                    y_ref[j, i * PIECE : (i + 1) * PIECE, g * WIDTH : (g + 1) * WIDTH]
                    for j in range(local)
                    for g in range(GROUPS)
                ],
                axis=0,
            ).astype(BF16)
            at = pl.ds(base + i * block_rows, block_rows)
            result_ref[at, :] = dot_nn(back, block).astype(BF16)
            if i % 4 == 3:
                number = len(stores)
                at = pl.ds(base + (i - 3) * block_rows, 4 * block_rows)
                stores.append(
                    pltpu.make_async_copy(
                        result_ref.at[at], result_hbm.at[at], result_sem.at[number]
                    )
                )
                stores[-1].start()
    for store in stores:
        store.wait()


def expert_call(rows, expert_in, expert_out):
    total = rows.shape[0]
    local = expert_in.shape[0]
    tokens = total // (2 * GROUPS * local)
    stores = total // (4 * local * GROUP_ROWS)
    return pl.pallas_call(
        expert_kernel,
        in_specs=[pl.BlockSpec(memory_space=pl.ANY)] * 3,
        out_specs=pl.BlockSpec(memory_space=pl.ANY),
        out_shape=jax.ShapeDtypeStruct((total, WIDTH), BF16),
        scratch_shapes=[
            pltpu.VMEM((total, WIDTH), BF16),
            pltpu.VMEM((total, WIDTH), BF16),
            pltpu.VMEM((local, tokens, D), BF16),
            pltpu.VMEM((local, tokens, D), F32),
            pltpu.VMEM((local, D, 2 * FF), BF16),
            pltpu.VMEM((local, FF, D), BF16),
            pltpu.SemaphoreType.DMA((2,)),
            pltpu.SemaphoreType.DMA((local,)),
            pltpu.SemaphoreType.DMA((local,)),
            pltpu.SemaphoreType.DMA((stores,)),
        ],
        compiler_params=params(),
        name="experts",
    )(rows, expert_in, expert_out)


def combine_kernel(code_ref, rows_ref, hidden_ref, out_ref, total_ref):
    step = pl.program_id(0)
    tile = rows_ref.shape[0]
    experts = code_ref.shape[1]
    at = iota((1, tile), 1)
    spread = (at // SPAN + step * (tile // SPAN) == iota((experts, tile), 0)).astype(BF16)
    both = dot_nn(code_ref[...], spread)
    code, gate = both[:TOK], both[TOK:].astype(BF16)
    slot, group = at % CAP, at // CAP % GROUPS
    zero = jnp.zeros((TOK, tile), BF16)
    weights = [
        jnp.where(code == jnp.where(group == g, slot, TOK).astype(F32), gate, zero)
        for g in range(GROUPS)
    ]
    part = dot_nn(jnp.concatenate(weights, axis=0), rows_ref[...])

    @pl.when(step == 0)
    def _():
        total_ref[...] = part

    @pl.when(step > 0)
    def _():
        total_ref[...] += part

    @pl.when(step == pl.num_programs(0) - 1)
    def _():
        for g in range(GROUPS):
            cut = slice(g * WIDTH, (g + 1) * WIDTH)
            mix = total_ref[g * TOK : (g + 1) * TOK, :]
            out_ref[:, cut] = (hidden_ref[:, cut].astype(F32) + mix).astype(BF16)


def combine_call(code, rows, hidden):
    total = rows.shape[0]
    steps = 4
    return pl.pallas_call(
        combine_kernel,
        grid=(steps,),
        in_specs=[
            pl.BlockSpec(code.shape, lambda i: (0, 0)),
            pl.BlockSpec((total // steps, WIDTH), lambda i: (i, 0)),
            pl.BlockSpec((TOK, D), lambda i: (0, 0)),
        ],
        out_specs=pl.BlockSpec((TOK, D), lambda i: (0, 0)),
        out_shape=jax.ShapeDtypeStruct((TOK, D), BF16),
        scratch_shapes=[pltpu.VMEM((GROUPS * TOK, WIDTH), F32)],
        compiler_params=params(),
        name="combine",
    )(code, rows, hidden)


def exchange(rows, axes):
    return lax.all_to_all(rows, axes, split_axis=0, concat_axis=0, tiled=True)


def per_device(
    queries,
    key_in,
    value_in,
    gate_in,
    residual_in,
    log_decay,
    beta_logit,
    lengths,
    head_gain,
    out_proj,
    post_gain,
    expert_in,
    expert_out,
    routes,
    route_gates,
):
    devices = lax.axis_size("dp") * lax.axis_size("ctx")
    local = expert_in.shape[0]
    shared = (key_in[0], value_in[0], log_decay[0], beta_logit[0])
    maps, solve = maps_call(lengths, *shared)
    query, inside = reads_call(lengths, queries[0], *shared, solve)
    code, code_t = route_call(routes[0], route_gates[0], local * devices)
    states = exchange(scan_call(exchange(maps, "ctx")), "ctx")
    hidden, sent = finish_call(
        states,
        query,
        inside,
        gate_in[0],
        residual_in[0],
        head_gain[None],
        post_gain[None],
        code_t,
        out_proj,
    )
    both = ("dp", "ctx")
    arrived = exchange(sent.reshape(devices, local * SPAN, WIDTH), both)
    results = expert_call(arrived.reshape(sent.shape), expert_in, expert_out)
    returned = exchange(results.reshape(devices, local * SPAN, WIDTH), both)
    return combine_call(code, returned.reshape(sent.shape), hidden)[None]


def solution(mesh):
    tokens = P("dp", "ctx", None)
    heads = P("dp", None, "ctx")
    experts = P(("dp", "ctx"), None, None)
    in_specs = (tokens,) * 5 + (heads, heads, P("dp", None), P(), P(), P())
    in_specs += (experts, experts, tokens, tokens)
    return jax.shard_map(
        per_device, mesh=mesh, in_specs=in_specs, out_specs=tokens, check_vma=False
    )
```

time: 281 us -> 266 us (0.947)
  blocking collectives: 32.7 us -> 197 us
  waiting for transfers between devices: 143 us -> 3.28 us
  starting transfers between devices: 26.2 us -> 4.12 us
  local copies, waits for them, and re-layouts: 13 us -> 2.28 us
  Pallas kernels: 64.7 us -> 58.8 us
    all_to_all x1 -> x3, blocking collectives: 32.7 us -> 197 us  [exchange(): return lax.all_to_all(rows, axes, split_axis=0, concat_axis=0, tiled=True)]
    all_to_all x5 -> x1, waiting for transfers between devices: 143 us -> 3.28 us  [exchange(): return lax.all_to_all(rows, axes, split_axis=0, concat_axis=0, tiled=True)]
    all_to_all x5 -> x1, starting transfers between devices: 26.2 us -> 4.12 us  [exchange(): return lax.all_to_all(rows, axes, split_axis=0, concat_axis=0, tiled=True)]
    unnamed x36 -> x8, local copies, waits for them, and re-layouts: 13 us -> 2.28 us
    pallas_call x9 -> x6, Pallas kernels: 60 us -> 52.6 us  [the longest x1 17.6 us: expert_call(): pl.pallas_call(expert_kernel, in_specs=[pl.BlockSpec(memory_space=pl.ANY)...]
  transfers between devices with their start and end apart: 5 -> 1, of which waited for: 5 -> 1; matrix products, arithmetic and copies ran while one was open for 0% -> 1% of each run, Pallas kernels for 12% -> 3%
where the time goes in v2:
time: 266 us; the launch traced here: 265 us
  blocking collectives  197 us (74%)
  Pallas kernels  58.8 us (22%)
  starting transfers between devices  4.12 us (2%)
  waiting for transfers between devices  3.28 us (1%)
    all_to_all x3, blocking collectives, exchange(): return lax.all_to_all(rows, axes, split_axis=0, concat_axis=0, tiled=True)  197 us
    pallas_call x1, Pallas kernels, expert_call(): pl.pallas_call(expert_kernel, in_specs=[pl.BlockSpec(memory_space=pl.ANY)...  17.6 us
    pallas_call x1, Pallas kernels, finish_call(): pl.pallas_call(finish_kernel, in_specs=[pl.BlockSpec(memory_space=pltpu.V...  10.4 us
    pallas_call x1, Pallas kernels, maps_call(): pl.pallas_call(maps_kernel, grid=(STEPS,), in_specs=[LENGTHS, KEY_BLOCK,...  9.7 us
    pallas_call x1, Pallas kernels, combine_call(): pl.pallas_call(combine_kernel, grid=(steps,), in_specs=[pl.BlockSpec(code...  8.03 us
    pallas_call x1, Pallas kernels, scan_call(): pl.pallas_call(scan_kernel, out_shape=jax.ShapeDtypeStruct((blocks * 64,...  6.2 us
  transfers between devices with their start and end apart: 1, of which 1 were waited for; matrix products, arithmetic and copies ran while one was open for 1% of the time, Pallas kernels for 3%

profile of v2, /device:TPU:1, one launch (start us, length us, event | category | flops | bytes accessed | tf_op | source)
XLA Modules:
  0.0 265.1 jit_solution(16913819304914220899)
XLA Ops:
  0.0 0.0 copy-start.1
  0.0 0.0 copy-start.2
  0.0 9.7 %block_maps.1 = (bf16[32,208,128]{2,1,0:T(8,128)(2,1)}, f32[16,128,128]{2,1,0:T(8,128)}) custom-call(s32[1,4]{1,0:T(1,128)} %len_ref.3, bf16[128,1024]{1,0:T(8,128)(2,1)} %bitcast.26, bf16[128,2048]{1,0:T(8,128)(2,1)} %bitcast.22, f32[16,128]{1,0:T(8,128)} %bitcast.33, f32[16,128]{1,0:T(8,128)} %bitcast.35), custom_call_target="tpu_custom_call" | custom-call | tf_op jit(solution)/shard_map/block_maps/pallas_call | solution.py:231
  9.7 32.8 %all_to_all.26.maps_ref = bf16[32,208,128]{2,1,0:T(8,128)(2,1)} all-to-all(bf16[32,208,128]{2,1,0:T(8,128)(2,1)} %get-tuple-element.15), channel_id=1, replica_groups=mesh['dp'=4,'ctx'=32] {'ctx'}, dimensions={0} | all-to-all | bytes 3407872 | tf_op jit(solution)/shard_map/all_to_all | solution.py:633
  42.5 6.2 %state_scan.1 = bf16[2048,128]{1,0:T(8,128)(2,1)} custom-call(bf16[32,208,128]{2,1,0:T(8,128)(2,1)} %all_to_all.26.maps_ref), custom_call_target="tpu_custom_call" | custom-call | tf_op jit(solution)/shard_map/state_scan/pallas_call | solution.py:287
  48.7 4.1 %all-to-all-start.1 = ((bf16[32,64,128]{2,1,0:T(8,128)(2,1)}), bf16[32,64,128]{2,1,0:T(8,128)(2,1)S(1)}, u32[]{:S(2)}, u32[]{:S(2)}) async-start(bf16[32,64,128]{2,1,0:T(8,128)(2,1)} %bitcast.24), calls=%async_computation.1 | async-start | bytes 1048576 | tf_op jit(solution)/shard_map/all_to_all | solution.py:633
  52.9 0.0 copy-done.1
  52.9 0.7 copy.16
  53.6 0.0 copy-done.2
  53.6 0.7 copy.17
  54.4 2.1 routing.1
  56.5 4.8 %block_reads.1 = (f32[16,128,128]{2,1,0:T(8,128)}, f32[128,2048]{1,0:T(8,128)}) custom-call(s32[1,4]{1,0:T(1,128)} %len_ref.3, bf16[128,1024]{1,0:T(8,128)(2,1)} %bitcast.30, bf16[128,1024]{1,0:T(8,128)(2,1)} %bitcast.27, bf16[128,2048]{1,0:T(8,128)(2,1)} %bitcast.23, f32[16,128]{1,0:T(8,128)} %bitcast.34, f32[16,128]{1,0:T(8,128)} %bitcast.36, ...), custom_call_target="tpu_custom_call" | custom-call | tf_op jit(solution)/shard_map/block_reads/pallas_call | solution.py:249
  61.2 3.3 %all-to-all-done.1 = bf16[32,64,128]{2,1,0:T(8,128)(2,1)S(1)} async-done(((bf16[32,64,128]{2,1,0:T(8,128)(2,1)}), bf16[32,64,128]{2,1,0:T(8,128)(2,1)S(1)}, u32[]{:S(2)}, u32[]{:S(2)}) %all-to-all-start.1) | async-done | bytes 524320 | tf_op jit(solution)/shard_map/all_to_all | solution.py:633
  64.5 0.0 copy-start
  64.5 0.8 copy-done
  65.3 10.4 %mixer_finish.1 = (bf16[128,2048]{1,0:T(8,128)(2,1)}, bf16[6144,512]{1,0:T(8,128)(2,1)}) custom-call(f32[1,128]{1,0:T(1,128)} %bitcast.38, f32[1,2048]{1,0:T(1,128)} %bitcast.37, f32[256,128]{1,0:T(8,128)} %get-tuple-element.14.code_ref, bf16[2048,128]{1,0:T(8,128)(2,1)} %bitcast.25, f32[16,128,128]{2,1,0:T(8,128)} %get-tuple-element.17.query_hbm, ...), custom_call_target="tpu_custom_call" | custom-call | tf_op jit(solution)/shard_map/mixer_finish/pallas_call | solution.py:404
  75.7 82.7 %all_to_all.27 = bf16[128,48,512]{2,1,0:T(8,128)(2,1)} all-to-all(bf16[128,48,512]{2,1,0:T(8,128)(2,1)} %bitcast.21), channel_id=1, replica_groups=mesh['dp'=4,'ctx'=32] {'dp','ctx'}, dimensions={0} | all-to-all | bytes 12582912 | tf_op jit(solution)/shard_map/all_to_all | solution.py:633
  158.4 17.6 %experts.1 = bf16[6144,512]{1,0:T(8,128)(2,1)} custom-call(bf16[6144,512]{1,0:T(8,128)(2,1)} %bitcast.19, bf16[2,2048,1024]{2,1,0:T(8,128)(2,1)} %in_hbm.1, bf16[2,512,2048]{2,1,0:T(8,128)(2,1)} %out_hbm.1), custom_call_target="tpu_custom_call" | custom-call | tf_op jit(solution)/shard_map/experts/pallas_call | solution.py:559
  176.0 81.0 %all_to_all.28 = bf16[128,48,512]{2,1,0:T(8,128)(2,1)} all-to-all(bf16[128,48,512]{2,1,0:T(8,128)(2,1)} %bitcast.20), channel_id=1, replica_groups=mesh['dp'=4,'ctx'=32] {'dp','ctx'}, dimensions={0} | all-to-all | bytes 12582912 | tf_op jit(solution)/shard_map/all_to_all | solution.py:633
  257.1 8.0 %combine.1 = bf16[128,2048]{1,0:T(8,128)(2,1)} custom-call(bf16[256,256]{1,0:T(8,128)(2,1)} %get-tuple-element.13.code_ref, bf16[6144,512]{1,0:T(8,128)(2,1)} %bitcast.18, bf16[128,2048]{1,0:T(8,128)(2,1)} %get-tuple-element.20.hidden_ref), custom_call_target="tpu_custom_call" | custom-call | tf_op jit(solution)/shard_map/combine/pallas_call | solution.py:616
Async XLA Ops:
  0.0 52.9 %copy-start.1 = (s32[1,128,10]{1,0,2:T(1,128)S(1)}, s32[1,128,10]{1,0,2:T(1,128)}, u32[]{:S(2)}) copy-start(s32[1,128,10]{1,0,2:T(1,128)} %param.28) | copy-start | bytes 15364
  0.0 53.6 %copy-start.2 = (f32[1,128,10]{1,0,2:T(1,128)S(1)}, f32[1,128,10]{1,0,2:T(1,128)}, u32[]{:S(2)}) copy-start(f32[1,128,10]{1,0,2:T(1,128)} %param.29) | copy-start | bytes 15364
  48.7 15.8 %all-to-all-start.1 = ((bf16[32,64,128]{2,1,0:T(8,128)(2,1)}), bf16[32,64,128]{2,1,0:T(8,128)(2,1)S(1)}, u32[]{:S(2)}, u32[]{:S(2)}) async-start(bf16[32,64,128]{2,1,0:T(8,128)(2,1)} %bitcast.24), calls=%async_computation.1 | async-start | bytes 1048576 | tf_op jit(solution)/shard_map/all_to_all | solution.py:633
  64.5 0.8 copy-start

commit v3 on v2

--- a/solution.py
+++ b/solution.py
@@ -21,12 +21,13 @@
 
 F32 = jnp.float32
 BF16 = jnp.bfloat16
-HEADS_STEP = 8
-MAP_ROWS = 64 + 128 + 16
+HEADS_STEP = 16
+MAP_ROWS = DV + DK + 16
 SRC_GROUP = 4
 GROUP_ROWS = SRC_GROUP * SPAN
 PIECE = SRC_GROUP * CAP
 DISPATCH_STEPS = 8
+COMBINE_PARTS = 2
 MIB = 1 << 20
 
 
@@ -174,10 +175,9 @@
                 jnp.where(at_row == 2, keep_low.astype(F32), 0.0),
             ),
         ).astype(BF16)
-        for s in range(2):
-            maps_ref[2 * h + s, 0:64, :] = offset[h][s * 64 : (s + 1) * 64]
-            maps_ref[2 * h + s, 64:192, :] = change[h]
-            maps_ref[2 * h + s, 192:208, :] = terms
+        maps_ref[h, 0:DV, :] = offset[h]
+        maps_ref[h, DV : DV + DK, :] = change[h]
+        maps_ref[h, DV + DK :, :] = terms
 
 
 def reads_kernel(
@@ -211,12 +211,11 @@
     for h in heads:
         local_ref[:, h * DV : (h + 1) * DV] = dot_nn(
             wide(mixed[h] * beta_row[h : h + 1]), twice(value[h], 0)
-        )
+        ).astype(BF16)
     for h in heads:
         enter_col = jnp.where(enters, jnp.exp(cum_col[h]), 0.0) * query_col[h // 2]
-        query_ref[h] = enter_col * query_f[h // 2] - dot_nn(
-            wide(mixed[h] * weight_row[h]), key_pair[h // 2]
-        )
+        read = dot_nn(wide(mixed[h] * weight_row[h]), key_pair[h // 2])
+        query_ref[h] = (enter_col * query_f[h // 2] - read).astype(BF16)
 
 
 STEPS = HV // HEADS_STEP
@@ -233,11 +232,11 @@
         grid=(STEPS,),
         in_specs=[LENGTHS, KEY_BLOCK, VALUE_BLOCK, HEAD_BLOCK, HEAD_BLOCK],
         out_specs=[
-            pl.BlockSpec((2 * HEADS_STEP, MAP_ROWS, DK), lambda i: (i, 0, 0)),
+            pl.BlockSpec((HEADS_STEP, MAP_ROWS, DK), lambda i: (i, 0, 0)),
             SQUARE_BLOCK,
         ],
         out_shape=[
-            jax.ShapeDtypeStruct((2 * HV, MAP_ROWS, DK), BF16),
+            jax.ShapeDtypeStruct((HV, MAP_ROWS, DK), BF16),
             jax.ShapeDtypeStruct((HV, TOK, TOK), F32),
         ],
         compiler_params=params(),
@@ -260,36 +259,37 @@
         ],
         out_specs=[SQUARE_BLOCK, VALUE_BLOCK],
         out_shape=[
-            jax.ShapeDtypeStruct((HV, TOK, DK), F32),
-            jax.ShapeDtypeStruct((TOK, HV * DV), F32),
+            jax.ShapeDtypeStruct((HV, TOK, DK), BF16),
+            jax.ShapeDtypeStruct((TOK, HV * DV), BF16),
         ],
         compiler_params=params(),
         name="block_reads",
     )(lengths, queries, key_in, value_in, log_decay, beta_logit, solve)
 
 
-def scan_kernel(maps_ref, out_ref):
-    blocks = maps_ref.shape[0]
-    state = jnp.zeros((64, DK), F32)
-    for at in range(blocks):
-        high, low = halves(state)
-        out_ref[at * 64 : (at + 1) * 64, :] = high
-        if at < blocks - 1:
-            offset = maps_ref[at, 0:64, :].astype(F32)
-            change = maps_ref[at, 64:192, :]
-            keep = jnp.sum(maps_ref[at, 192:208, :].astype(F32), 0, keepdims=True)
-            moved = dot_nn(jnp.concatenate([high, low], axis=0), change)
-            state = keep * state - (moved[:64] + moved[64:]) + offset
-
-
-def scan_call(maps):
-    blocks = maps.shape[0]
+def scan_kernel(own_ref, other_ref, out_ref):
+    chips = own_ref.shape[0]
+    even = lax.axis_index("ctx") % 2 == 0
+    state = jnp.zeros((DV, DK), F32)
+    for chip in range(chips):
+        own, other = own_ref[chip], other_ref[chip]
+        entering = []
+        for block in (jnp.where(even, own, other), jnp.where(even, other, own)):
+            high, low = halves(state)
+            entering.append(high)
+            keep = jnp.sum(block[DV + DK :].astype(F32), 0, keepdims=True)
+            moved = dot_nn(jnp.concatenate([high, low], axis=0), block[DV : DV + DK])
+            state = keep * state + block[:DV].astype(F32) - (moved[:DV] + moved[DV:])
+        out_ref[chip * DV : (chip + 1) * DV, :] = jnp.where(even, entering[0], entering[1])
+
+
+def scan_call(own, other):
     return pl.pallas_call(
         scan_kernel,
-        out_shape=jax.ShapeDtypeStruct((blocks * 64, DK), BF16),
-        compiler_params=params(),
+        out_shape=jax.ShapeDtypeStruct((own.shape[0] * DV, DK), BF16),
+        compiler_params=params(24 * MIB),
         name="state_scan",
-    )(maps)
+    )(own, other)
 
 
 def finish_kernel(
@@ -346,7 +346,7 @@
     normed = []
     for h in range(HV):
         cut = slice(h * DV, (h + 1) * DV)
-        outputs = local_ref[:, cut] + dot_nt(wide(query_ref[h]), twice(state_ref[cut, :], 1))
+        outputs = local_ref[:, cut].astype(F32) + dot_nt(query_ref[h], state_ref[cut, :])
         scale = lax.rsqrt(jnp.mean(outputs * outputs, -1, keepdims=True) + EPSILON)
         gate = gate_ref[:, cut].astype(F32)
         normed.append((outputs * scale * gain * (gate / (1.0 + jnp.exp(-gate)))).astype(BF16))
@@ -423,21 +423,22 @@
 
 def route_kernel(routes_ref, gates_ref, code_ref, code_t_ref):
     experts = code_t_ref.shape[0]
-    expert = iota((TOK, experts), 1)
-    hit = jnp.zeros((TOK, experts), F32)
-    gate = jnp.zeros((TOK, experts), F32)
+    expert = iota((experts, TOK), 0)
+    hit = jnp.zeros((experts, TOK), F32)
+    gate = jnp.zeros((experts, TOK), F32)
     for k in range(TOPK):
-        match = routes_ref[:, k : k + 1] == expert
+        match = routes_ref[k : k + 1, :] == expert
         hit = jnp.where(match, 1.0, hit)
-        gate = jnp.where(match, gates_ref[:, k : k + 1], gate)
+        gate = jnp.where(match, gates_ref[k : k + 1, :], gate)
     square = (TOK, TOK)
-    before = (iota(square, 0) > iota(square, 1)).astype(BF16)
-    rank = dot_nn(before, hit.astype(BF16))
+    before = (iota(square, 0) < iota(square, 1)).astype(BF16)
+    rank = dot_nn(hit.astype(BF16), before)
     code = jnp.where(hit > 0.0, rank, -1.0)
-    code_ref[0:TOK, :] = code.astype(BF16)
-    code_ref[TOK:, :] = gate.astype(BF16)
+    code_t_ref[...] = code
     for at in range(0, experts, TOK):
-        code_t_ref[at : at + TOK, :] = code[:, at : at + TOK].T
+        cut = slice(at, at + TOK)
+        code_ref[0:TOK, cut] = code[cut].T.astype(BF16)
+        code_ref[TOK:, cut] = gate[cut].T.astype(BF16)
 
 
 def route_call(routes, gates, experts):
@@ -450,6 +451,35 @@
         compiler_params=params(),
         name="routing",
     )(routes, gates)
+
+
+def block_orders(local):
+    block_rows = local * GROUP_ROWS
+    square = (block_rows, block_rows)
+    to_at, from_at = iota(square, 0), iota(square, 1)
+
+    def source_of(at):
+        piece, rest = at // PIECE, at % PIECE
+        return (rest // CAP) * (local * SPAN) + piece * CAP + rest % CAP
+
+    order = (source_of(to_at) == from_at).astype(BF16)
+    back = (source_of(from_at) == to_at).astype(BF16)
+    return order, back
+
+
+def unpack_blocks(order, rows_ref, base, count, local, x_ref):
+    block_rows = local * GROUP_ROWS
+    for i in range(0, count, 2):
+        moved = [
+            dot_nn(order, rows_ref[base + k * block_rows : base + (k + 1) * block_rows, :])
+            for k in (i, i + 1)
+        ]
+        for j in range(local):
+            for g in range(GROUPS):
+                cut = slice((j * GROUPS + g) * PIECE, (j * GROUPS + g + 1) * PIECE)
+                x_ref[j, i * PIECE : (i + 2) * PIECE, g * WIDTH : (g + 1) * WIDTH] = (
+                    jnp.concatenate([m[cut] for m in moved], axis=0).astype(BF16)
+                )
 
 
 def expert_kernel(
@@ -493,30 +523,12 @@
 
     block_rows = local * GROUP_ROWS
     count = half // block_rows
-    square = (block_rows, block_rows)
-    to_at, from_at = iota(square, 0), iota(square, 1)
-
-    def source_of(at):
-        piece, rest = at // PIECE, at % PIECE
-        return (rest // CAP) * (local * SPAN) + piece * CAP + rest % CAP
-
-    order = (source_of(to_at) == from_at).astype(BF16)
-    back = (source_of(from_at) == to_at).astype(BF16)
+    order, back = block_orders(local)
     stores = []
     for part in range(2):
         base = part * half
         halves_in[part].wait()
-        for i in range(0, count, 2):
-            moved = [
-                dot_nn(order, rows_ref[base + k * block_rows : base + (k + 1) * block_rows, :])
-                for k in (i, i + 1)
-            ]
-            for j in range(local):
-                for g in range(GROUPS):
-                    cut = slice((j * GROUPS + g) * PIECE, (j * GROUPS + g + 1) * PIECE)
-                    x_ref[j, i * PIECE : (i + 2) * PIECE, g * WIDTH : (g + 1) * WIDTH] = (
-                        jnp.concatenate([m[cut] for m in moved], axis=0).astype(BF16)
-                    )
+        unpack_blocks(order, rows_ref, base, count, local, x_ref)
         for j in range(local):
             x = x_ref[j]
             if part == 0:
@@ -578,59 +590,55 @@
     )(rows, expert_in, expert_out)
 
 
-def combine_kernel(code_ref, rows_ref, hidden_ref, out_ref, total_ref):
-    step = pl.program_id(0)
-    tile = rows_ref.shape[0]
+def combine_kernel(code_ref, hidden_ref, rows_hbm, out_ref, rows_ref, x_ref, sems):
+    parts, local, tokens, width = x_ref.shape
     experts = code_ref.shape[1]
-    at = iota((1, tile), 1)
-    spread = (at // SPAN + step * (tile // SPAN) == iota((experts, tile), 0)).astype(BF16)
-    both = dot_nn(code_ref[...], spread)
-    code, gate = both[:TOK], both[TOK:].astype(BF16)
-    slot, group = at % CAP, at // CAP % GROUPS
-    zero = jnp.zeros((TOK, tile), BF16)
-    weights = [
-        jnp.where(code == jnp.where(group == g, slot, TOK).astype(F32), gate, zero)
-        for g in range(GROUPS)
-    ]
-    part = dot_nn(jnp.concatenate(weights, axis=0), rows_ref[...])
-
-    @pl.when(step == 0)
-    def _():
-        total_ref[...] = part
-
-    @pl.when(step > 0)
-    def _():
-        total_ref[...] += part
-
-    @pl.when(step == pl.num_programs(0) - 1)
-    def _():
-        for g in range(GROUPS):
-            cut = slice(g * WIDTH, (g + 1) * WIDTH)
-            mix = total_ref[g * TOK : (g + 1) * TOK, :]
-            out_ref[:, cut] = (hidden_ref[:, cut].astype(F32) + mix).astype(BF16)
-
-
-def combine_call(code, rows, hidden):
-    total = rows.shape[0]
-    steps = 4
+    part_rows = rows_ref.shape[0] // parts
+    loads = []
+    for part in range(parts):
+        at = pl.ds(part * part_rows, part_rows)
+        loads.append(pltpu.make_async_copy(rows_hbm.at[at], rows_ref.at[at], sems.at[part]))
+        loads[-1].start()
+    order, unused = block_orders(local)
+    at = iota((1, local * tokens), 1)
+    slot = (at % CAP).astype(F32)
+    owner = (at % tokens) // CAP * local + at // tokens
+    total = hidden_ref[...].astype(F32)
+    for part in range(parts):
+        first = part * (tokens // CAP) * local
+        spread = (owner + first == iota((experts, local * tokens), 0)).astype(BF16)
+        both = dot_nn(code_ref[...], spread)
+        weights = jnp.where(both[:TOK] == slot, both[TOK:], 0.0).astype(BF16)
+        loads[part].wait()
+        count = part_rows // (local * GROUP_ROWS)
+        unpack_blocks(order, rows_ref, part * part_rows, count, local, x_ref.at[part])
+        total = total + dot_nn(weights, x_ref[part].reshape(local * tokens, width))
+    out_ref[...] = total.astype(BF16)
+
+
+def combine_call(code, rows, hidden, local):
+    parts = COMBINE_PARTS
+    tokens = rows.shape[0] // (parts * local * GROUPS)
     return pl.pallas_call(
         combine_kernel,
-        grid=(steps,),
-        in_specs=[
-            pl.BlockSpec(code.shape, lambda i: (0, 0)),
-            pl.BlockSpec((total // steps, WIDTH), lambda i: (i, 0)),
-            pl.BlockSpec((TOK, D), lambda i: (0, 0)),
-        ],
-        out_specs=pl.BlockSpec((TOK, D), lambda i: (0, 0)),
+        in_specs=[pl.BlockSpec(memory_space=pltpu.VMEM)] * 2
+        + [pl.BlockSpec(memory_space=pl.ANY)],
+        out_specs=pl.BlockSpec(memory_space=pltpu.VMEM),
         out_shape=jax.ShapeDtypeStruct((TOK, D), BF16),
-        scratch_shapes=[pltpu.VMEM((GROUPS * TOK, WIDTH), F32)],
+        scratch_shapes=[
+            pltpu.VMEM(rows.shape, BF16),
+            pltpu.VMEM((parts, local, tokens, D), BF16),
+            pltpu.SemaphoreType.DMA((parts,)),
+        ],
         compiler_params=params(),
         name="combine",
-    )(code, rows, hidden)
-
-
-def exchange(rows, axes):
-    return lax.all_to_all(rows, axes, split_axis=0, concat_axis=0, tiled=True)
+    )(code, hidden, rows)
+
+
+def exchange(rows, axes, groups=None):
+    return lax.all_to_all(
+        rows, axes, split_axis=0, concat_axis=0, tiled=True, axis_index_groups=groups
+    )
 
 
 def per_device(
@@ -655,8 +663,12 @@
     shared = (key_in[0], value_in[0], log_decay[0], beta_logit[0])
     maps, solve = maps_call(lengths, *shared)
     query, inside = reads_call(lengths, queries[0], *shared, solve)
-    code, code_t = route_call(routes[0], route_gates[0], local * devices)
-    states = exchange(scan_call(exchange(maps, "ctx")), "ctx")
+    code, code_t = route_call(routes[0].T, route_gates[0].T, local * devices)
+    blocks = lax.axis_size("ctx")
+    cores = [list(range(core, blocks, 2)) for core in range(2)]
+    own = exchange(maps, "ctx", cores)
+    other = lax.ppermute(own, "ctx", [(i, i ^ 1) for i in range(blocks)])
+    states = exchange(scan_call(own, other), "ctx", cores)
     hidden, sent = finish_call(
         states,
         query,
@@ -672,7 +684,7 @@
     arrived = exchange(sent.reshape(devices, local * SPAN, WIDTH), both)
     results = expert_call(arrived.reshape(sent.shape), expert_in, expert_out)
     returned = exchange(results.reshape(devices, local * SPAN, WIDTH), both)
-    return combine_call(code, returned.reshape(sent.shape), hidden)[None]
+    return combine_call(code, returned.reshape(sent.shape), hidden, local)[None]
 
 
 def solution(mesh):

time: 266 us -> 257 us (0.966)
  blocking collectives: 197 us -> 189 us
  Pallas kernels: 58.8 us -> 53.4 us
    all_to_all x3, blocking collectives: 197 us -> 189 us  [exchange(): lax.all_to_all(rows, axes, split_axis=0, concat_axis=0, tiled=True, axis_...]
  transfers between devices with their start and end apart: 1 -> 2, of which waited for: 1 -> 2; matrix products, arithmetic and copies ran while one was open for 1% -> 0% of each run, Pallas kernels for 3% -> 2%
where the time goes in v3:
time: 257 us; the launch traced here: 256 us
  blocking collectives  189 us (74%)
  Pallas kernels  53.4 us (21%)
  waiting for transfers between devices  5.83 us (2%)
  starting transfers between devices  5.7 us (2%)
    all_to_all x3, blocking collectives, exchange(): lax.all_to_all(rows, axes, split_axis=0, concat_axis=0, tiled=True, axis_...  189 us
    pallas_call x1, Pallas kernels, expert_call(): pl.pallas_call(expert_kernel, in_specs=[pl.BlockSpec(memory_space=pl.ANY)...  17.6 us
    pallas_call x1, Pallas kernels, finish_call(): pl.pallas_call(finish_kernel, in_specs=[pl.BlockSpec(memory_space=pltpu.V...  10 us
    pallas_call x1, Pallas kernels, maps_call(): pl.pallas_call(maps_kernel, grid=(STEPS,), in_specs=[LENGTHS, KEY_BLOCK,...  7.74 us
    pallas_call x1, Pallas kernels, combine_call(): pl.pallas_call(combine_kernel, in_specs=[pl.BlockSpec(memory_space=pltpu....  6.92 us
  transfers between devices with their start and end apart: 2, of which 2 were waited for; matrix products, arithmetic and copies ran while one was open for 0% of the time, Pallas kernels for 2%

profile of v3, /device:TPU:1, one launch (start us, length us, event | category | flops | bytes accessed | tf_op | source)
XLA Modules:
  0.0 256.0 jit_solution(2257660793099200764)
XLA Ops:
  0.0 0.0 copy-start.1
  0.0 0.0 copy-start.2
  0.0 7.7 %block_maps.1 = (bf16[16,272,128]{2,1,0:T(8,128)(2,1)}, f32[16,128,128]{2,1,0:T(8,128)}) custom-call(s32[1,4]{1,0:T(1,128)} %len_ref.3, bf16[128,1024]{1,0:T(8,128)(2,1)} %bitcast.33, bf16[128,2048]{1,0:T(8,128)(2,1)} %bitcast.30, f32[16,128]{1,0:T(8,128)} %bitcast.38, f32[16,128]{1,0:T(8,128)} %bitcast.40), custom_call_target="tpu_custom_call" | custom-call | tf_op jit(solution)/shard_map/block_maps/pallas_call | solution.py:230
  7.7 24.5 %all_to_all.26.own_ref = bf16[16,272,128]{2,1,0:T(8,128)(2,1)S(1)} all-to-all(bf16[16,272,128]{2,1,0:T(8,128)(2,1)} %get-tuple-element.15), channel_id=1, replica_groups={{0,2,4,6,8,10,12,14,16,18,20,22,24,26,28,30},{1,3,5,7,9,11,13,15,17,19,..., dimensions={0} | all-to-all | bytes 2228224 | tf_op jit(solution)/shard_map/all_to_all | solution.py:639
  32.2 2.0 collective-permute-start
  34.2 2.4 collective-permute-done.other_ref
  36.5 5.0 %state_scan.1 = bf16[2048,128]{1,0:T(8,128)(2,1)} custom-call(bf16[16,272,128]{2,1,0:T(8,128)(2,1)S(1)} %all_to_all.26.own_ref, bf16[16,272,128]{2,1,0:T(8,128)(2,1)S(1)} %collective-permute-done.other_ref), custom_call_target="tpu_custom_call" | custom-call | tf_op jit(solution)/shard_map/state_scan/pallas_call | solution.py:287
  41.6 3.8 %all-to-all-start.1 = ((bf16[16,128,128]{2,1,0:T(8,128)(2,1)}), bf16[16,128,128]{2,1,0:T(8,128)(2,1)S(1)}, u32[]{:S(2)}, u32[]{:S(2)}) async-start(bf16[16,128,128]{2,1,0:T(8,128)(2,1)} %bitcast.8), calls=%async_computation.1 | async-start | bytes 1048576 | tf_op jit(solution)/shard_map/all_to_all | solution.py:639
  45.3 0.0 copy-done.1
  45.3 0.6 copy.21
  45.9 0.0 copy-done.2
  45.9 0.6 copy.20
  46.5 1.7 routing.1
  48.3 4.4 %block_reads.1 = (bf16[16,128,128]{2,1,0:T(8,128)(2,1)}, bf16[128,2048]{1,0:T(8,128)(2,1)}) custom-call(s32[1,4]{1,0:T(1,128)} %len_ref.3, bf16[128,1024]{1,0:T(8,128)(2,1)} %bitcast.37, bf16[128,1024]{1,0:T(8,128)(2,1)} %bitcast.34, bf16[128,2048]{1,0:T(8,128)(2,1)} %bitcast.31, f32[16,128]{1,0:T(8,128)} %bitcast.39, f32[16,128]{1,0:T(8,128)} %bitcast.41, ...), custom_call_target="tpu_custom_call" | custom-call | tf_op jit(solution)/shard_map/block_reads/pallas_call | solution.py:248
  52.6 3.5 %all-to-all-done.1 = bf16[16,128,128]{2,1,0:T(8,128)(2,1)S(1)} async-done(((bf16[16,128,128]{2,1,0:T(8,128)(2,1)}), bf16[16,128,128]{2,1,0:T(8,128)(2,1)S(1)}, u32[]{:S(2)}, u32[]{:S(2)}) %all-to-all-start.1) | async-done | bytes 524320 | tf_op jit(solution)/shard_map/all_to_all | solution.py:639
  56.1 0.0 copy-start
  56.1 0.8 copy-done
  56.9 10.0 %mixer_finish.1 = (bf16[128,2048]{1,0:T(8,128)(2,1)}, bf16[6144,512]{1,0:T(8,128)(2,1)}) custom-call(f32[1,128]{1,0:T(1,128)} %bitcast.45, f32[1,2048]{1,0:T(1,128)} %bitcast.44, f32[256,128]{1,0:T(8,128)} %get-tuple-element.14.code_ref, bf16[2048,128]{1,0:T(8,128)(2,1)} %bitcast.32, bf16[16,128,128]{2,1,0:T(8,128)(2,1)} %get-tuple-element.17.query_hbm, ...), custom_call_target="tpu_custom_call" | custom-call | tf_op jit(solution)/shard_map/mixer_finish/pallas_call | solution.py:404
  66.9 83.1 %all_to_all.27 = bf16[128,48,512]{2,1,0:T(8,128)(2,1)} all-to-all(bf16[128,48,512]{2,1,0:T(8,128)(2,1)} %bitcast.29), channel_id=1, replica_groups=mesh['dp'=4,'ctx'=32] {'dp','ctx'}, dimensions={0} | all-to-all | bytes 12582912 | tf_op jit(solution)/shard_map/all_to_all | solution.py:639
  150.0 17.6 %experts.1 = bf16[6144,512]{1,0:T(8,128)(2,1)} custom-call(bf16[6144,512]{1,0:T(8,128)(2,1)} %bitcast.27, bf16[2,2048,1024]{2,1,0:T(8,128)(2,1)} %in_hbm.1, bf16[2,512,2048]{2,1,0:T(8,128)(2,1)} %out_hbm.1), custom_call_target="tpu_custom_call" | custom-call | tf_op jit(solution)/shard_map/experts/pallas_call | solution.py:571
  167.6 81.3 %all_to_all.28 = bf16[128,48,512]{2,1,0:T(8,128)(2,1)} all-to-all(bf16[128,48,512]{2,1,0:T(8,128)(2,1)} %bitcast.28), channel_id=1, replica_groups=mesh['dp'=4,'ctx'=32] {'dp','ctx'}, dimensions={0} | all-to-all | bytes 12582912 | tf_op jit(solution)/shard_map/all_to_all | solution.py:639
  248.9 6.9 %combine.1 = bf16[128,2048]{1,0:T(8,128)(2,1)} custom-call(bf16[256,256]{1,0:T(8,128)(2,1)} %get-tuple-element.13.code_ref, bf16[128,2048]{1,0:T(8,128)(2,1)} %get-tuple-element.19.hidden_ref, bf16[6144,512]{1,0:T(8,128)(2,1)} %bitcast.26), custom_call_target="tpu_custom_call" | custom-call | tf_op jit(solution)/shard_map/combine/pallas_call | solution.py:622
Async XLA Ops:
  0.0 45.3 %copy-start.1 = (s32[1,128,10]{1,0,2:T(1,128)S(1)}, s32[1,128,10]{1,0,2:T(1,128)}, u32[]{:S(2)}) copy-start(s32[1,128,10]{1,0,2:T(1,128)} %param.28) | copy-start | bytes 15364
  0.0 45.9 %copy-start.2 = (f32[1,128,10]{1,0,2:T(1,128)S(1)}, f32[1,128,10]{1,0,2:T(1,128)}, u32[]{:S(2)}) copy-start(f32[1,128,10]{1,0,2:T(1,128)} %param.29) | copy-start | bytes 15364
  32.2 4.3 %collective-permute-start = (bf16[16,272,128]{2,1,0:T(8,128)(2,1)S(1)}, bf16[16,272,128]{2,1,0:T(8,128)(2,1)S(1)}, u32[]{:S(2)}, u32[]{:S(2)}) collective-permute-start(bf16[16,272,128]{2,1,0:T(8,128)(2,1)S(1)} %all_to_all.26.own_ref), channel_id=1, source_target_pairs={{0,1},{1,0},{2,3},{3,2},{4,5},{5,4},{6,7},{7,6},{8,9},{9,8},{10,11... | collective-permute-start | bytes 3342344 | tf_op jit(solution)/shard_map/ppermute | solution.py:670
  41.6 14.5 %all-to-all-start.1 = ((bf16[16,128,128]{2,1,0:T(8,128)(2,1)}), bf16[16,128,128]{2,1,0:T(8,128)(2,1)S(1)}, u32[]{:S(2)}, u32[]{:S(2)}) async-start(bf16[16,128,128]{2,1,0:T(8,128)(2,1)} %bitcast.8), calls=%async_computation.1 | async-start | bytes 1048576 | tf_op jit(solution)/shard_map/all_to_all | solution.py:639
  56.1 0.8 copy-start

commit v4 on v3

--- a/solution.py
+++ b/solution.py
@@ -296,14 +296,6 @@
     gain_ref,
     post_ref,
     code_ref,
-    state_hbm,
-    query_hbm,
-    local_hbm,
-    gate_hbm,
-    resid_hbm,
-    proj_hbm,
-    hidden_hbm,
-    out_hbm,
     state_ref,
     query_ref,
     local_ref,
@@ -311,37 +303,9 @@
     resid_ref,
     weight_ref,
     hidden_ref,
+    out_ref,
     rows_ref,
-    out_ref,
-    sems,
-    weight_sems,
-    hidden_sem,
-    out_sems,
 ):
-    loads = [
-        pltpu.make_async_copy(source, target, sems.at[i])
-        for i, (source, target) in enumerate(
-            [
-                (state_hbm, state_ref),
-                (query_hbm, query_ref),
-                (local_hbm, local_ref),
-                (gate_hbm, gate_ref),
-                (resid_hbm, resid_ref),
-            ]
-        )
-    ]
-    quarters = []
-    for g in range(GROUPS):
-        at = (slice(None), pl.ds(g * WIDTH, WIDTH))
-        quarters.append(
-            pltpu.make_async_copy(proj_hbm.at[at], weight_ref.at[at], weight_sems.at[g])
-        )
-    for load in loads:
-        load.start()
-    quarters[0].start()
-    for load in loads:
-        load.wait()
-    quarters[1].start()
     gain = gain_ref[...]
     normed = []
     for h in range(HV):
@@ -355,24 +319,18 @@
     parts = []
     for g in range(GROUPS):
         cut = slice(g * WIDTH, (g + 1) * WIDTH)
-        quarters[g].wait()
-        if g + 2 < GROUPS:
-            quarters[g + 2].start()
         mixed = dot_nn(normed, weight_ref[:, cut])
         hidden = (resid_ref[:, cut].astype(F32) + mixed).astype(BF16)
         hidden_ref[:, cut] = hidden
         hidden = hidden.astype(F32)
         total = total + jnp.sum(hidden * hidden, -1, keepdims=True)
         parts.append(hidden)
-    keep = pltpu.make_async_copy(hidden_ref, hidden_hbm, hidden_sem)
-    keep.start()
     scale = lax.rsqrt(total / D + EPSILON)
     for g in range(GROUPS):
         cut = slice(g * WIDTH, (g + 1) * WIDTH)
         rows_ref[g * TOK : (g + 1) * TOK, :] = (parts[g] * scale * post_ref[:, cut]).astype(BF16)
 
     count = code_ref.shape[0] // DISPATCH_STEPS
-    stores = [keep]
     for step in range(DISPATCH_STEPS):
         code = code_ref[step * count : (step + 1) * count, :][:, None, :]
         tiles = []
@@ -389,36 +347,24 @@
             tiles.append(dot_nn(jnp.concatenate(pick, axis=1), source).reshape(count, 1, 8, WIDTH))
         at = pl.ds(step * count * SPAN, count * SPAN)
         out_ref[at, :] = jnp.concatenate(tiles, axis=1).reshape(count * SPAN, WIDTH).astype(BF16)
-        stores.append(pltpu.make_async_copy(out_ref.at[at], out_hbm.at[at], out_sems.at[step]))
-        stores[-1].start()
-    for store in stores:
-        store.wait()
 
 
 def finish_call(state, query, local, gate_in, residual_in, head_gain, post_gain, code_t, out_proj):
     experts = code_t.shape[0]
-    large = [state, query, local, gate_in, residual_in]
     hidden = jax.ShapeDtypeStruct((TOK, D), BF16)
     sent = jax.ShapeDtypeStruct((experts * SPAN, WIDTH), BF16)
     rows = jax.ShapeDtypeStruct((GROUPS * TOK, WIDTH), BF16)
     return pl.pallas_call(
         finish_kernel,
-        in_specs=[pl.BlockSpec(memory_space=pltpu.VMEM)] * 3
-        + [pl.BlockSpec(memory_space=pl.ANY)] * 6,
-        out_specs=[pl.BlockSpec(memory_space=pl.ANY)] * 2,
+        in_specs=[pl.BlockSpec(memory_space=pltpu.VMEM)] * 9,
+        out_specs=[pl.BlockSpec(memory_space=pltpu.VMEM)] * 2,
         out_shape=[hidden, sent],
-        scratch_shapes=[
-            pltpu.VMEM(x.shape, x.dtype) for x in large + [out_proj, hidden, rows, sent]
-        ]
-        + [
-            pltpu.SemaphoreType.DMA((len(large),)),
-            pltpu.SemaphoreType.DMA((GROUPS,)),
-            pltpu.SemaphoreType.DMA,
-            pltpu.SemaphoreType.DMA((DISPATCH_STEPS,)),
-        ],
-        compiler_params=params(),
+        scratch_shapes=[pltpu.VMEM(rows.shape, BF16)],
+        compiler_params=params(24 * MIB),
         name="mixer_finish",
-    )(head_gain, post_gain, code_t, *large, out_proj)
+    )(
+        head_gain, post_gain, code_t, state, query, local, gate_in, residual_in, out_proj
+    )
 
 
 def route_kernel(routes_ref, gates_ref, code_ref, code_t_ref):
@@ -482,63 +428,21 @@
                 )
 
 
-def expert_kernel(
-    rows_hbm,
-    in_hbm,
-    out_hbm,
-    result_hbm,
-    rows_ref,
-    result_ref,
-    x_ref,
-    y_ref,
-    in_vmem,
-    out_vmem,
-    row_sem,
-    in_sem,
-    out_sem,
-    result_sem,
-):
-    local = in_vmem.shape[0]
-    total = rows_ref.shape[0]
-    half = total // 2
-    halves_in = []
-    for part in range(2):
-        at = pl.ds(part * half, half)
-        halves_in.append(
-            pltpu.make_async_copy(rows_hbm.at[at], rows_ref.at[at], row_sem.at[part])
-        )
-    loads = []
-    for j in range(local):
-        loads.append(
-            (
-                pltpu.make_async_copy(in_hbm.at[j], in_vmem.at[j], in_sem.at[j]),
-                pltpu.make_async_copy(out_hbm.at[j], out_vmem.at[j], out_sem.at[j]),
-            )
-        )
-    halves_in[0].start()
-    for first, second in loads:
-        first.start()
-        second.start()
-    halves_in[1].start()
-
+def expert_kernel(rows_ref, in_ref, out_ref, result_ref, x_ref, y_ref):
+    local = in_ref.shape[0]
+    half = rows_ref.shape[0] // 2
     block_rows = local * GROUP_ROWS
     count = half // block_rows
     order, back = block_orders(local)
-    stores = []
     for part in range(2):
         base = part * half
-        halves_in[part].wait()
         unpack_blocks(order, rows_ref, base, count, local, x_ref)
         for j in range(local):
             x = x_ref[j]
-            if part == 0:
-                loads[j][0].wait()
-            gate = dot_nn(x, in_vmem[j, :, :FF])
-            up = dot_nn(x, in_vmem[j, :, FF:])
+            gate = dot_nn(x, in_ref[j, :, :FF])
+            up = dot_nn(x, in_ref[j, :, FF:])
             hidden = (gate / (1.0 + jnp.exp(-gate)) * up).astype(BF16)
-            if part == 0:
-                loads[j][1].wait()
-            y_ref[j] = dot_nn(hidden, out_vmem[j])
+            y_ref[j] = dot_nn(hidden, out_ref[j])
         for i in range(count):
             block = jnp.concatenate(
                 [
@@ -550,55 +454,30 @@
             ).astype(BF16)
             at = pl.ds(base + i * block_rows, block_rows)
             result_ref[at, :] = dot_nn(back, block).astype(BF16)
-            if i % 4 == 3:
-                number = len(stores)
-                at = pl.ds(base + (i - 3) * block_rows, 4 * block_rows)
-                stores.append(
-                    pltpu.make_async_copy(
-                        result_ref.at[at], result_hbm.at[at], result_sem.at[number]
-                    )
-                )
-                stores[-1].start()
-    for store in stores:
-        store.wait()
 
 
 def expert_call(rows, expert_in, expert_out):
     total = rows.shape[0]
     local = expert_in.shape[0]
     tokens = total // (2 * GROUPS * local)
-    stores = total // (4 * local * GROUP_ROWS)
     return pl.pallas_call(
         expert_kernel,
-        in_specs=[pl.BlockSpec(memory_space=pl.ANY)] * 3,
-        out_specs=pl.BlockSpec(memory_space=pl.ANY),
+        in_specs=[pl.BlockSpec(memory_space=pltpu.VMEM)] * 3,
+        out_specs=pl.BlockSpec(memory_space=pltpu.VMEM),
         out_shape=jax.ShapeDtypeStruct((total, WIDTH), BF16),
         scratch_shapes=[
-            pltpu.VMEM((total, WIDTH), BF16),
-            pltpu.VMEM((total, WIDTH), BF16),
             pltpu.VMEM((local, tokens, D), BF16),
             pltpu.VMEM((local, tokens, D), F32),
-            pltpu.VMEM((local, D, 2 * FF), BF16),
-            pltpu.VMEM((local, FF, D), BF16),
-            pltpu.SemaphoreType.DMA((2,)),
-            pltpu.SemaphoreType.DMA((local,)),
-            pltpu.SemaphoreType.DMA((local,)),
-            pltpu.SemaphoreType.DMA((stores,)),
-        ],
-        compiler_params=params(),
+        ],
+        compiler_params=params(28 * MIB),
         name="experts",
     )(rows, expert_in, expert_out)
 
 
-def combine_kernel(code_ref, hidden_ref, rows_hbm, out_ref, rows_ref, x_ref, sems):
+def combine_kernel(code_ref, hidden_ref, rows_ref, out_ref, x_ref):
     parts, local, tokens, width = x_ref.shape
     experts = code_ref.shape[1]
     part_rows = rows_ref.shape[0] // parts
-    loads = []
-    for part in range(parts):
-        at = pl.ds(part * part_rows, part_rows)
-        loads.append(pltpu.make_async_copy(rows_hbm.at[at], rows_ref.at[at], sems.at[part]))
-        loads[-1].start()
     order, unused = block_orders(local)
     at = iota((1, local * tokens), 1)
     slot = (at % CAP).astype(F32)
@@ -609,7 +488,6 @@
         spread = (owner + first == iota((experts, local * tokens), 0)).astype(BF16)
         both = dot_nn(code_ref[...], spread)
         weights = jnp.where(both[:TOK] == slot, both[TOK:], 0.0).astype(BF16)
-        loads[part].wait()
         count = part_rows // (local * GROUP_ROWS)
         unpack_blocks(order, rows_ref, part * part_rows, count, local, x_ref.at[part])
         total = total + dot_nn(weights, x_ref[part].reshape(local * tokens, width))
@@ -621,16 +499,13 @@
     tokens = rows.shape[0] // (parts * local * GROUPS)
     return pl.pallas_call(
         combine_kernel,
-        in_specs=[pl.BlockSpec(memory_space=pltpu.VMEM)] * 2
-        + [pl.BlockSpec(memory_space=pl.ANY)],
+        in_specs=[pl.BlockSpec(memory_space=pltpu.VMEM)] * 3,
         out_specs=pl.BlockSpec(memory_space=pltpu.VMEM),
         out_shape=jax.ShapeDtypeStruct((TOK, D), BF16),
         scratch_shapes=[
-            pltpu.VMEM(rows.shape, BF16),
             pltpu.VMEM((parts, local, tokens, D), BF16),
-            pltpu.SemaphoreType.DMA((parts,)),
-        ],
-        compiler_params=params(),
+        ],
+        compiler_params=params(32 * MIB),
         name="combine",
     )(code, hidden, rows)
 
@@ -667,6 +542,9 @@
     blocks = lax.axis_size("ctx")
     cores = [list(range(core, blocks, 2)) for core in range(2)]
     own = exchange(maps, "ctx", cores)
+    own, query, inside, code, code_t = lax.optimization_barrier(
+        (own, query, inside, code, code_t)
+    )
     other = lax.ppermute(own, "ctx", [(i, i ^ 1) for i in range(blocks)])
     states = exchange(scan_call(own, other), "ctx", cores)
     hidden, sent = finish_call(

time: 257 us -> 246 us (0.957)
  Pallas kernels: 53.4 us -> 39.9 us
  blocking collectives: 189 us -> 176 us
  local copies, waits for them, and re-layouts: 1.99 us -> 8.97 us
  starting transfers between devices: 5.7 us -> 10.3 us
  waiting for transfers between devices: 5.83 us -> 10.4 us
    all_to_all x3, blocking collectives: 189 us -> 176 us  [exchange(): lax.all_to_all(rows, axes, split_axis=0, concat_axis=0, tiled=True, axis_...]
    unnamed x8 -> x26, local copies, waits for them, and re-layouts: 1.99 us -> 8.97 us
    pallas_call x1, Pallas kernels: 10 us -> 4.05 us  [finish_call(): pl.pallas_call(finish_kernel, in_specs=[pl.BlockSpec(memory_space=pltpu.V...]
    all_to_all x1, waiting for transfers between devices: 3.45 us -> 8.03 us  [exchange(): lax.all_to_all(rows, axes, split_axis=0, concat_axis=0, tiled=True, axis_...]
    pallas_call x1, Pallas kernels: 17.6 us -> 13.8 us  [expert_call(): pl.pallas_call(expert_kernel, in_specs=[pl.BlockSpec(memory_space=pltpu.V...]
    all_to_all x1, starting transfers between devices: 3.75 us -> 7.59 us  [exchange(): lax.all_to_all(rows, axes, split_axis=0, concat_axis=0, tiled=True, axis_...]
    pallas_call x1, Pallas kernels: 6.92 us -> 3.9 us  [combine_call(): pl.pallas_call(combine_kernel, in_specs=[pl.BlockSpec(memory_space=pltpu....]
  transfers between devices with their start and end apart: 2 -> 2, of which waited for: 2 -> 2; matrix products, arithmetic and copies ran while one was open for 0% -> 1% of each run, Pallas kernels for 2% -> 2%
where the time goes in v4:
time: 246 us; the launch traced here: 245 us
  blocking collectives  176 us (72%)
  Pallas kernels  39.9 us (16%)
  waiting for transfers between devices  10.4 us (4%)
  starting transfers between devices  10.3 us (4%)
  local copies, waits for them, and re-layouts  8.97 us (4%)
    all_to_all x3, blocking collectives, exchange(): lax.all_to_all(rows, axes, split_axis=0, concat_axis=0, tiled=True, axis_...  176 us
    pallas_call x1, Pallas kernels, expert_call(): pl.pallas_call(expert_kernel, in_specs=[pl.BlockSpec(memory_space=pltpu.V...  13.8 us
    unnamed x26, local copies, waits for them, and re-layouts  8.97 us
    all_to_all x1, waiting for transfers between devices, exchange(): lax.all_to_all(rows, axes, split_axis=0, concat_axis=0, tiled=True, axis_...  8.03 us
    pallas_call x1, Pallas kernels, maps_call(): pl.pallas_call(maps_kernel, grid=(STEPS,), in_specs=[LENGTHS, KEY_BLOCK,...  7.83 us
    all_to_all x1, starting transfers between devices, exchange(): lax.all_to_all(rows, axes, split_axis=0, concat_axis=0, tiled=True, axis_...  7.59 us
  transfers between devices with their start and end apart: 2, of which 2 were waited for; matrix products, arithmetic and copies ran while one was open for 1% of the time, Pallas kernels for 2%

profile of v4, /device:TPU:1, one launch (start us, length us, event | category | flops | bytes accessed | tf_op | source)
XLA Modules:
  0.0 245.4 jit_solution(15520452272343139153)
XLA Ops:
  0.0 0.0 copy-start.8
  0.0 0.0 copy-start.9
  0.0 0.0 copy-start.3
  0.0 0.0 copy-start.2
  0.0 7.8 %block_maps.1 = (bf16[16,272,128]{2,1,0:T(8,128)(2,1)}, f32[16,128,128]{2,1,0:T(8,128)}) custom-call(s32[1,4]{1,0:T(1,128)} %len_ref.3, bf16[128,1024]{1,0:T(8,128)(2,1)} %bitcast.40, bf16[128,2048]{1,0:T(8,128)(2,1)} %bitcast.38, f32[16,128]{1,0:T(8,128)} %bitcast.43, f32[16,128]{1,0:T(8,128)} %bitcast.45), custom_call_target="tpu_custom_call" | custom-call | tf_op jit(solution)/shard_map/block_maps/pallas_call | solution.py:230
  7.8 7.6 %all-to-all-start = ((bf16[16,272,128]{2,1,0:T(8,128)(2,1)}), bf16[16,272,128]{2,1,0:T(8,128)(2,1)S(1)}, u32[]{:S(2)}, u32[]{:S(2)}) async-start(bf16[16,272,128]{2,1,0:T(8,128)(2,1)} %get-tuple-element.18), calls=%async_computation | async-start | bytes 2228224 | tf_op jit(solution)/shard_map/all_to_all | solution.py:514
  15.4 1.3 copy.21
  16.7 1.3 copy.20
  18.0 1.8 routing.1
  19.8 4.3 %block_reads.1 = (bf16[16,128,128]{2,1,0:T(8,128)(2,1)}, bf16[128,2048]{1,0:T(8,128)(2,1)}) custom-call(s32[1,4]{1,0:T(1,128)} %len_ref.3, bf16[128,1024]{1,0:T(8,128)(2,1)} %bitcast.42, bf16[128,1024]{1,0:T(8,128)(2,1)} %bitcast.41, bf16[128,2048]{1,0:T(8,128)(2,1)} %bitcast.39, f32[16,128]{1,0:T(8,128)} %bitcast.44, f32[16,128]{1,0:T(8,128)} %bitcast.46, ...), custom_call_target="tpu_custom_call" | custom-call | tf_op jit(solution)/shard_map/block_reads/pallas_call | solution.py:248
  24.1 8.0 %all-to-all-done.own_ref = bf16[16,272,128]{2,1,0:T(8,128)(2,1)S(1)} async-done(((bf16[16,272,128]{2,1,0:T(8,128)(2,1)}), bf16[16,272,128]{2,1,0:T(8,128)(2,1)S(1)}, u32[]{:S(2)}, u32[]{:S(2)}) %all-to-all-start) | async-done | bytes 1114144 | tf_op jit(solution)/shard_map/all_to_all | solution.py:514
  32.1 2.7 %collective-permute-start = (bf16[16,272,128]{2,1,0:T(8,128)(2,1)S(1)}, bf16[16,272,128]{2,1,0:T(8,128)(2,1)S(1)}, u32[]{:S(2)}, u32[]{:S(2)}) collective-permute-start(bf16[16,272,128]{2,1,0:T(8,128)(2,1)S(1)} %all-to-all-done.own_ref), channel_id=1, source_target_pairs={{0,1},{1,0},{2,3},{3,2},{4,5},{5,4},{6,7},{7,6},{8,9},{9,8},{10,11... | collective-permute-start | bytes 3342344 | tf_op jit(solution)/shard_map/ppermute | solution.py:548
  34.8 2.4 collective-permute-done.other_ref
  37.2 4.2 %state_scan.1 = bf16[2048,128]{1,0:T(8,128)(2,1)S(1)} custom-call(bf16[16,272,128]{2,1,0:T(8,128)(2,1)S(1)} %all-to-all-done.own_ref, bf16[16,272,128]{2,1,0:T(8,128)(2,1)S(1)} %collective-permute-done.other_ref), custom_call_target="tpu_custom_call" | custom-call | tf_op jit(solution)/shard_map/state_scan/pallas_call | solution.py:287
  41.4 13.5 %all_to_all.26 = bf16[16,128,128]{2,1,0:T(8,128)(2,1)S(1)} all-to-all(bf16[16,128,128]{2,1,0:T(8,128)(2,1)S(1)} %bitcast.33), channel_id=1, replica_groups={{0,2,4,6,8,10,12,14,16,18,20,22,24,26,28,30},{1,3,5,7,9,11,13,15,17,19,..., dimensions={0} | all-to-all | bytes 1048576 | tf_op jit(solution)/shard_map/all_to_all | solution.py:514
  55.0 0.0 copy-done.8
  55.0 0.0 copy-done.9
  55.0 0.0 copy-done.3
  55.0 0.0 copy-done.2
  55.0 0.0 copy-start
  55.0 3.4 %copy-done = bf16[2048,2048]{1,0:T(8,128)(2,1)S(1)} copy-done((bf16[2048,2048]{1,0:T(8,128)(2,1)S(1)}, bf16[2048,2048]{1,0:T(8,128)(2,1)}, u32[]{:S(2)}) %copy-start) | copy-done | bytes 8388632
  58.4 0.0 copy-start.4
  58.4 1.0 copy-done.4
  59.4 0.0 copy-start.5
  59.4 1.0 copy-done.5
  60.5 0.0 copy-start.7
  60.5 0.9 copy-done.7
  61.4 0.0 slice-start
  61.4 4.1 %mixer_finish.1 = (bf16[128,2048]{1,0:T(8,128)(2,1)S(1)}, bf16[6144,512]{1,0:T(8,128)(2,1)S(1)}) custom-call(f32[1,128]{1,0:T(1,128)S(1)} %bitcast.37, f32[1,2048]{1,0:T(1,128)S(1)} %bitcast.36, f32[256,128]{1,0:T(8,128)S(1)} %copy-done.7, bf16[2048,128]{1,0:T(8,128)(2,1)S(1)} %bitcast.32, bf16[16,128,128]{2,1,0:T(8,128)(2,1)S(1)} %copy-done.4, ...), custom_call_target="tpu_custom_call" | custom-call | tf_op jit(solution)/shard_map/mixer_finish/pallas_call | solution.py:357
  65.4 0.0 slice-start.1
  65.5 0.0 copy-start.1
  65.5 82.8 %all_to_all.27 = bf16[128,48,512]{2,1,0:T(8,128)(2,1)S(1)} all-to-all(bf16[128,48,512]{2,1,0:T(8,128)(2,1)S(1)} %bitcast.31), channel_id=1, replica_groups=mesh['dp'=4,'ctx'=32] {'dp','ctx'}, dimensions={0} | all-to-all | bytes 12582912 | tf_op jit(solution)/shard_map/all_to_all | solution.py:514
  148.3 0.0 slice-done
  148.3 0.0 slice-done.1
  148.3 0.0 copy-done.1
  148.3 13.8 %experts.1 = bf16[6144,512]{1,0:T(8,128)(2,1)S(1)} custom-call(bf16[6144,512]{1,0:T(8,128)(2,1)S(1)} %bitcast.27, bf16[2,2048,1024]{2,1,0:T(8,128)(2,1)S(1)} %bitcast.30, bf16[2,512,2048]{2,1,0:T(8,128)(2,1)S(1)} %copy-done.1), custom_call_target="tpu_custom_call" | custom-call | tf_op jit(solution)/shard_map/experts/pallas_call | solution.py:463
  162.0 0.0 copy-start.6
  162.1 79.5 %all_to_all.28 = bf16[128,48,512]{2,1,0:T(8,128)(2,1)S(1)} all-to-all(bf16[128,48,512]{2,1,0:T(8,128)(2,1)S(1)} %bitcast.28), channel_id=1, replica_groups=mesh['dp'=4,'ctx'=32] {'dp','ctx'}, dimensions={0} | all-to-all | bytes 12582912 | tf_op jit(solution)/shard_map/all_to_all | solution.py:514
  241.5 0.0 copy-done.6
  241.5 3.9 %combine.1 = bf16[128,2048]{1,0:T(8,128)(2,1)} custom-call(bf16[256,256]{1,0:T(8,128)(2,1)S(1)} %copy-done.6, bf16[128,2048]{1,0:T(8,128)(2,1)S(1)} %get-tuple-element.29.hidden_ref, bf16[6144,512]{1,0:T(8,128)(2,1)S(1)} %bitcast.26), custom_call_target="tpu_custom_call" | custom-call | tf_op jit(solution)/shard_map/combine/pallas_call | solution.py:500
  (1 shorter events, 0.0 us)
Async XLA Ops:
  0.0 55.0 %copy-start.8 = (f32[2048]{0:T(1024)S(1)}, f32[2048]{0:T(1024)}, u32[]{:S(2)}) copy-start(f32[2048]{0:T(1024)} %param.25) | copy-start | bytes 24580
  0.0 55.0 %copy-start.9 = (f32[128]{0:T(128)S(1)}, f32[128]{0:T(128)}, u32[]{:S(2)}) copy-start(f32[128]{0:T(128)} %param.23) | copy-start | bytes 1540
  0.0 55.0 %copy-start.3 = (bf16[1,128,2048]{2,1,0:T(8,128)(2,1)S(1)}, bf16[1,128,2048]{2,1,0:T(8,128)(2,1)}, u32[]{:S(2)}) copy-start(bf16[1,128,2048]{2,1,0:T(8,128)(2,1)} %param.19) | copy-start | bytes 1572868
  0.0 55.0 %copy-start.2 = (bf16[1,128,2048]{2,1,0:T(8,128)(2,1)S(1)}, bf16[1,128,2048]{2,1,0:T(8,128)(2,1)}, u32[]{:S(2)}) copy-start(bf16[1,128,2048]{2,1,0:T(8,128)(2,1)} %param.18) | copy-start | bytes 1572868
  7.8 24.3 %all-to-all-start = ((bf16[16,272,128]{2,1,0:T(8,128)(2,1)}), bf16[16,272,128]{2,1,0:T(8,128)(2,1)S(1)}, u32[]{:S(2)}, u32[]{:S(2)}) async-start(bf16[16,272,128]{2,1,0:T(8,128)(2,1)} %get-tuple-element.18), calls=%async_computation | async-start | bytes 2228224 | tf_op jit(solution)/shard_map/all_to_all | solution.py:514
  32.1 5.1 %collective-permute-start = (bf16[16,272,128]{2,1,0:T(8,128)(2,1)S(1)}, bf16[16,272,128]{2,1,0:T(8,128)(2,1)S(1)}, u32[]{:S(2)}, u32[]{:S(2)}) collective-permute-start(bf16[16,272,128]{2,1,0:T(8,128)(2,1)S(1)} %all-to-all-done.own_ref), channel_id=1, source_target_pairs={{0,1},{1,0},{2,3},{3,2},{4,5},{5,4},{6,7},{7,6},{8,9},{9,8},{10,11... | collective-permute-start | bytes 3342344 | tf_op jit(solution)/shard_map/ppermute | solution.py:548
  55.0 3.4 %copy-start = (bf16[2048,2048]{1,0:T(8,128)(2,1)S(1)}, bf16[2048,2048]{1,0:T(8,128)(2,1)}, u32[]{:S(2)}) copy-start(bf16[2048,2048]{1,0:T(8,128)(2,1)} %weight_ref.1) | copy-start | bytes 25165828
  58.4 1.0 copy-start.4
  59.4 1.0 copy-start.5
  60.5 0.9 copy-start.7
  61.4 86.9 %slice-start = ((s8[8388608]{0:T(1024)(128)(4,1)}), s8[4194304]{0:T(1024)(128)(4,1)S(1)}, s32[]{:S(2)}) async-start(s8[8388608]{0:T(1024)(128)(4,1)} %bitcast.29), calls=%async_computation.4 | async-start | bytes 8388608
  65.4 82.8 %slice-start.1 = ((s8[8388608]{0:T(1024)(128)(4,1)}), s8[4194304]{0:T(1024)(128)(4,1)S(1)}, s32[]{:S(2)}) async-start(s8[8388608]{0:T(1024)(128)(4,1)} %bitcast.29), calls=%async_computation.5 | async-start | bytes 8388608
  65.5 82.8 %copy-start.1 = (bf16[2,512,2048]{2,1,0:T(8,128)(2,1)S(1)}, bf16[2,512,2048]{2,1,0:T(8,128)(2,1)}, u32[]{:S(2)}) copy-start(bf16[2,512,2048]{2,1,0:T(8,128)(2,1)} %out_ref.1) | copy-start | bytes 12582916
  162.0 79.5 %copy-start.6 = (bf16[256,256]{1,0:T(8,128)(2,1)S(1)}, bf16[256,256]{1,0:T(8,128)(2,1)}, u32[]{:S(2)}) copy-start(bf16[256,256]{1,0:T(8,128)(2,1)} %get-tuple-element.24.code_ref) | copy-start | bytes 393220

commit v5 on v4

--- a/solution.py
+++ b/solution.py
@@ -288,6 +288,9 @@
         scan_kernel,
         out_shape=jax.ShapeDtypeStruct((own.shape[0] * DV, DK), BF16),
         compiler_params=params(24 * MIB),
+        cost_estimate=pl.CostEstimate(
+            flops=6 * 10**9, bytes_accessed=4 * 10**6, transcendentals=0
+        ),
         name="state_scan",
     )(own, other)
 
@@ -297,15 +300,35 @@
     post_ref,
     code_ref,
     state_ref,
+    weight_ref,
+    query_hbm,
+    local_hbm,
+    gate_hbm,
+    resid_hbm,
+    hidden_ref,
+    out_ref,
+    rows_ref,
     query_ref,
     local_ref,
     gate_ref,
     resid_ref,
-    weight_ref,
-    hidden_ref,
-    out_ref,
-    rows_ref,
+    sems,
 ):
+    loads = [
+        pltpu.make_async_copy(source, target, sems.at[i])
+        for i, (source, target) in enumerate(
+            [
+                (query_hbm, query_ref),
+                (local_hbm, local_ref),
+                (gate_hbm, gate_ref),
+                (resid_hbm, resid_ref),
+            ]
+        )
+    ]
+    for load in loads:
+        load.start()
+    for load in loads:
+        load.wait()
     gain = gain_ref[...]
     normed = []
     for h in range(HV):
@@ -356,15 +379,17 @@
     rows = jax.ShapeDtypeStruct((GROUPS * TOK, WIDTH), BF16)
     return pl.pallas_call(
         finish_kernel,
-        in_specs=[pl.BlockSpec(memory_space=pltpu.VMEM)] * 9,
+        in_specs=[pl.BlockSpec(memory_space=pltpu.VMEM)] * 5
+        + [pl.BlockSpec(memory_space=pl.ANY)] * 4,
         out_specs=[pl.BlockSpec(memory_space=pltpu.VMEM)] * 2,
         out_shape=[hidden, sent],
-        scratch_shapes=[pltpu.VMEM(rows.shape, BF16)],
+        scratch_shapes=[
+            pltpu.VMEM(x.shape, x.dtype) for x in [rows, query, local, gate_in, residual_in]
+        ]
+        + [pltpu.SemaphoreType.DMA((4,))],
         compiler_params=params(24 * MIB),
         name="mixer_finish",
-    )(
-        head_gain, post_gain, code_t, state, query, local, gate_in, residual_in, out_proj
-    )
+    )(head_gain, post_gain, code_t, state, out_proj, query, local, gate_in, residual_in)
 
 
 def route_kernel(routes_ref, gates_ref, code_ref, code_t_ref):

time: 246 us -> 240 us (0.976)
  local copies, waits for them, and re-layouts: 8.97 us -> 2.64 us
    unnamed x26 -> x28, local copies, waits for them, and re-layouts: 8.97 us -> 2.64 us
  transfers between devices with their start and end apart: 2 -> 2, of which waited for: 2 -> 2; matrix products, arithmetic and copies ran while one was open for 1% -> 1% of each run, Pallas kernels for 2% -> 3%
where the time goes in v5:
time: 240 us; the launch traced here: 239 us
  blocking collectives  176 us (73%)
  Pallas kernels  39.7 us (17%)
  starting transfers between devices  10.4 us (4%)
  waiting for transfers between devices  10.4 us (4%)
  local copies, waits for them, and re-layouts  2.64 us (1%)
    all_to_all x3, blocking collectives, exchange(): lax.all_to_all(rows, axes, split_axis=0, concat_axis=0, tiled=True, axis_...  176 us
    pallas_call x1, Pallas kernels, expert_call(): pl.pallas_call(expert_kernel, in_specs=[pl.BlockSpec(memory_space=pltpu.V...  13.6 us
    all_to_all x1, waiting for transfers between devices, exchange(): lax.all_to_all(rows, axes, split_axis=0, concat_axis=0, tiled=True, axis_...  8.04 us
    pallas_call x1, Pallas kernels, maps_call(): pl.pallas_call(maps_kernel, grid=(STEPS,), in_specs=[LENGTHS, KEY_BLOCK,...  7.76 us
    all_to_all x1, starting transfers between devices, exchange(): lax.all_to_all(rows, axes, split_axis=0, concat_axis=0, tiled=True, axis_...  7.59 us
  transfers between devices with their start and end apart: 2, of which 2 were waited for; matrix products, arithmetic and copies ran while one was open for 1% of the time, Pallas kernels for 3%

profile of v5, /device:TPU:1, one launch (start us, length us, event | category | flops | bytes accessed | tf_op | source)
XLA Modules:
  0.0 239.1 jit_solution(7367164596709700073)
XLA Ops:
  0.0 7.8 %block_maps.1 = (bf16[16,272,128]{2,1,0:T(8,128)(2,1)}, f32[16,128,128]{2,1,0:T(8,128)}) custom-call(s32[1,4]{1,0:T(1,128)} %len_ref.3, bf16[128,1024]{1,0:T(8,128)(2,1)} %bitcast.42, bf16[128,2048]{1,0:T(8,128)(2,1)} %bitcast.40, f32[16,128]{1,0:T(8,128)} %bitcast.45, f32[16,128]{1,0:T(8,128)} %bitcast.47), custom_call_target="tpu_custom_call" | custom-call | tf_op jit(solution)/shard_map/block_maps/pallas_call | solution.py:230
  7.8 7.6 %all-to-all-start = ((bf16[16,272,128]{2,1,0:T(8,128)(2,1)}), bf16[16,272,128]{2,1,0:T(8,128)(2,1)S(1)}, u32[]{:S(2)}, u32[]{:S(2)}) async-start(bf16[16,272,128]{2,1,0:T(8,128)(2,1)} %get-tuple-element.18), calls=%async_computation | async-start | bytes 2228224 | tf_op jit(solution)/shard_map/all_to_all | solution.py:539
  15.4 1.3 copy.21
  16.6 1.3 copy.20
  17.9 1.7 routing.1
  19.7 4.3 %block_reads.1 = (bf16[16,128,128]{2,1,0:T(8,128)(2,1)}, bf16[128,2048]{1,0:T(8,128)(2,1)}) custom-call(s32[1,4]{1,0:T(1,128)} %len_ref.3, bf16[128,1024]{1,0:T(8,128)(2,1)} %bitcast.44, bf16[128,1024]{1,0:T(8,128)(2,1)} %bitcast.43, bf16[128,2048]{1,0:T(8,128)(2,1)} %bitcast.41, f32[16,128]{1,0:T(8,128)} %bitcast.46, f32[16,128]{1,0:T(8,128)} %bitcast.48, ...), custom_call_target="tpu_custom_call" | custom-call | tf_op jit(solution)/shard_map/block_reads/pallas_call | solution.py:248
  24.0 8.0 %all-to-all-done.own_ref = bf16[16,272,128]{2,1,0:T(8,128)(2,1)S(1)} async-done(((bf16[16,272,128]{2,1,0:T(8,128)(2,1)}), bf16[16,272,128]{2,1,0:T(8,128)(2,1)S(1)}, u32[]{:S(2)}, u32[]{:S(2)}) %all-to-all-start) | async-done | bytes 1114144 | tf_op jit(solution)/shard_map/all_to_all | solution.py:539
  32.0 0.0 slice-start.2
  32.1 0.0 slice-start.3
  32.1 0.0 copy-start.1
  32.1 0.0 copy-start.2
  32.1 0.0 copy-start.3
  32.1 0.0 copy-start.4
  32.1 0.0 copy-start.6
  32.1 0.0 copy-start.7
  32.1 0.0 copy-start.8
  32.1 2.8 %collective-permute-start = (bf16[16,272,128]{2,1,0:T(8,128)(2,1)S(1)}, bf16[16,272,128]{2,1,0:T(8,128)(2,1)S(1)}, u32[]{:S(2)}, u32[]{:S(2)}) collective-permute-start(bf16[16,272,128]{2,1,0:T(8,128)(2,1)S(1)} %all-to-all-done.own_ref), channel_id=1, source_target_pairs={{0,1},{1,0},{2,3},{3,2},{4,5},{5,4},{6,7},{7,6},{8,9},{9,8},{10,11... | collective-permute-start | bytes 3342344 | tf_op jit(solution)/shard_map/ppermute | solution.py:573
  34.9 2.4 collective-permute-done.other_ref
  37.3 4.2 %state_scan.1 = bf16[2048,128]{1,0:T(8,128)(2,1)S(1)} custom-call(bf16[16,272,128]{2,1,0:T(8,128)(2,1)S(1)} %all-to-all-done.own_ref, bf16[16,272,128]{2,1,0:T(8,128)(2,1)S(1)} %collective-permute-done.other_ref), custom_call_target="tpu_custom_call" | custom-call | flops 6000000000 | bytes 4000000 | tf_op jit(solution)/shard_map/state_scan/pallas_call | solution.py:287
  41.5 13.5 %all_to_all.26 = bf16[16,128,128]{2,1,0:T(8,128)(2,1)S(1)} all-to-all(bf16[16,128,128]{2,1,0:T(8,128)(2,1)S(1)} %bitcast.37), channel_id=1, replica_groups={{0,2,4,6,8,10,12,14,16,18,20,22,24,26,28,30},{1,3,5,7,9,11,13,15,17,19,..., dimensions={0} | all-to-all | bytes 1048576 | tf_op jit(solution)/shard_map/all_to_all | solution.py:539
  55.0 0.0 slice-done.2
  55.0 0.0 slice-done.3
  55.1 0.0 copy-done.1
  55.1 0.0 copy-done.2
  55.1 0.0 copy-done.3
  55.1 0.0 copy-done.4
  55.1 0.0 copy-done.6
  55.1 0.0 copy-done.7
  55.1 0.0 copy-done.8
  55.1 0.0 slice-start
  55.1 4.2 %mixer_finish.1 = (bf16[128,2048]{1,0:T(8,128)(2,1)S(1)}, bf16[6144,512]{1,0:T(8,128)(2,1)S(1)}) custom-call(f32[1,128]{1,0:T(1,128)S(1)} %bitcast.39, f32[1,2048]{1,0:T(1,128)S(1)} %bitcast.38, f32[256,128]{1,0:T(8,128)S(1)} %copy-done.6, bf16[2048,128]{1,0:T(8,128)(2,1)S(1)} %bitcast.34, bf16[2048,2048]{1,0:T(8,128)(2,1)S(1)} %bitcast.32, ...), custom_call_target="tpu_custom_call" | custom-call | tf_op jit(solution)/shard_map/mixer_finish/pallas_call | solution.py:380
  59.3 0.0 slice-start.1
  59.3 0.0 copy-start
  59.3 82.8 %all_to_all.27 = bf16[128,48,512]{2,1,0:T(8,128)(2,1)S(1)} all-to-all(bf16[128,48,512]{2,1,0:T(8,128)(2,1)S(1)} %bitcast.33), channel_id=1, replica_groups=mesh['dp'=4,'ctx'=32] {'dp','ctx'}, dimensions={0} | all-to-all | bytes 12582912 | tf_op jit(solution)/shard_map/all_to_all | solution.py:539
  142.1 0.0 slice-done
  142.1 0.0 slice-done.1
  142.1 0.0 copy-done
  142.1 13.6 %experts.1 = bf16[6144,512]{1,0:T(8,128)(2,1)S(1)} custom-call(bf16[6144,512]{1,0:T(8,128)(2,1)S(1)} %bitcast.27, bf16[2,2048,1024]{2,1,0:T(8,128)(2,1)S(1)} %bitcast.30, bf16[2,512,2048]{2,1,0:T(8,128)(2,1)S(1)} %copy-done), custom_call_target="tpu_custom_call" | custom-call | tf_op jit(solution)/shard_map/experts/pallas_call | solution.py:488
  155.8 0.0 copy-start.5
  155.8 79.5 %all_to_all.28 = bf16[128,48,512]{2,1,0:T(8,128)(2,1)S(1)} all-to-all(bf16[128,48,512]{2,1,0:T(8,128)(2,1)S(1)} %bitcast.28), channel_id=1, replica_groups=mesh['dp'=4,'ctx'=32] {'dp','ctx'}, dimensions={0} | all-to-all | bytes 12582912 | tf_op jit(solution)/shard_map/all_to_all | solution.py:539
  235.2 0.0 copy-done.5
  235.2 3.9 %combine.1 = bf16[128,2048]{1,0:T(8,128)(2,1)} custom-call(bf16[256,256]{1,0:T(8,128)(2,1)S(1)} %copy-done.5, bf16[128,2048]{1,0:T(8,128)(2,1)S(1)} %get-tuple-element.29.hidden_ref, bf16[6144,512]{1,0:T(8,128)(2,1)S(1)} %bitcast.26), custom_call_target="tpu_custom_call" | custom-call | tf_op jit(solution)/shard_map/combine/pallas_call | solution.py:525
  (2 shorter events, 0.0 us)
Async XLA Ops:
  7.8 24.3 %all-to-all-start = ((bf16[16,272,128]{2,1,0:T(8,128)(2,1)}), bf16[16,272,128]{2,1,0:T(8,128)(2,1)S(1)}, u32[]{:S(2)}, u32[]{:S(2)}) async-start(bf16[16,272,128]{2,1,0:T(8,128)(2,1)} %get-tuple-element.18), calls=%async_computation | async-start | bytes 2228224 | tf_op jit(solution)/shard_map/all_to_all | solution.py:539
  32.0 23.0 %slice-start.2 = ((s8[8388608]{0:T(1024)(128)(4,1)}), s8[4194304]{0:T(1024)(128)(4,1)S(1)}, s32[]{:S(2)}) async-start(s8[8388608]{0:T(1024)(128)(4,1)} %bitcast.31), calls=%async_computation.6 | async-start | bytes 8388608
  32.1 23.0 %slice-start.3 = ((s8[8388608]{0:T(1024)(128)(4,1)}), s8[4194304]{0:T(1024)(128)(4,1)S(1)}, s32[]{:S(2)}) async-start(s8[8388608]{0:T(1024)(128)(4,1)} %bitcast.31), calls=%async_computation.7 | async-start | bytes 8388608
  32.1 23.0 %copy-start.1 = (bf16[1,128,2048]{2,1,0:T(8,128)(2,1)S(1)}, bf16[1,128,2048]{2,1,0:T(8,128)(2,1)}, u32[]{:S(2)}) copy-start(bf16[1,128,2048]{2,1,0:T(8,128)(2,1)} %param.18) | copy-start | bytes 1572868
  32.1 23.0 %copy-start.2 = (bf16[1,128,2048]{2,1,0:T(8,128)(2,1)S(1)}, bf16[1,128,2048]{2,1,0:T(8,128)(2,1)}, u32[]{:S(2)}) copy-start(bf16[1,128,2048]{2,1,0:T(8,128)(2,1)} %param.19) | copy-start | bytes 1572868
  32.1 23.0 %copy-start.3 = (bf16[16,128,128]{2,1,0:T(8,128)(2,1)S(1)}, bf16[16,128,128]{2,1,0:T(8,128)(2,1)}, u32[]{:S(2)}) copy-start(bf16[16,128,128]{2,1,0:T(8,128)(2,1)} %get-tuple-element.27.query_hbm) | copy-start | bytes 1572868
  32.1 23.0 %copy-start.4 = (bf16[128,2048]{1,0:T(8,128)(2,1)S(1)}, bf16[128,2048]{1,0:T(8,128)(2,1)}, u32[]{:S(2)}) copy-start(bf16[128,2048]{1,0:T(8,128)(2,1)} %get-tuple-element.28.local_hbm) | copy-start | bytes 1572868
  32.1 23.0 %copy-start.6 = (f32[256,128]{1,0:T(8,128)S(1)}, f32[256,128]{1,0:T(8,128)}, u32[]{:S(2)}) copy-start(f32[256,128]{1,0:T(8,128)} %get-tuple-element.25.code_ref) | copy-start | bytes 393220
  32.1 23.0 %copy-start.7 = (f32[2048]{0:T(1024)S(1)}, f32[2048]{0:T(1024)}, u32[]{:S(2)}) copy-start(f32[2048]{0:T(1024)} %param.25) | copy-start | bytes 24580
  32.1 23.0 %copy-start.8 = (f32[128]{0:T(128)S(1)}, f32[128]{0:T(128)}, u32[]{:S(2)}) copy-start(f32[128]{0:T(128)} %param.23) | copy-start | bytes 1540
  32.1 5.2 %collective-permute-start = (bf16[16,272,128]{2,1,0:T(8,128)(2,1)S(1)}, bf16[16,272,128]{2,1,0:T(8,128)(2,1)S(1)}, u32[]{:S(2)}, u32[]{:S(2)}) collective-permute-start(bf16[16,272,128]{2,1,0:T(8,128)(2,1)S(1)} %all-to-all-done.own_ref), channel_id=1, source_target_pairs={{0,1},{1,0},{2,3},{3,2},{4,5},{5,4},{6,7},{7,6},{8,9},{9,8},{10,11... | collective-permute-start | bytes 3342344 | tf_op jit(solution)/shard_map/ppermute | solution.py:573
  55.1 87.0 %slice-start = ((s8[8388608]{0:T(1024)(128)(4,1)}), s8[4194304]{0:T(1024)(128)(4,1)S(1)}, s32[]{:S(2)}) async-start(s8[8388608]{0:T(1024)(128)(4,1)} %bitcast.29), calls=%async_computation.4 | async-start | bytes 8388608
  59.3 82.8 %slice-start.1 = ((s8[8388608]{0:T(1024)(128)(4,1)}), s8[4194304]{0:T(1024)(128)(4,1)S(1)}, s32[]{:S(2)}) async-start(s8[8388608]{0:T(1024)(128)(4,1)} %bitcast.29), calls=%async_computation.5 | async-start | bytes 8388608
  59.3 82.8 %copy-start = (bf16[2,512,2048]{2,1,0:T(8,128)(2,1)S(1)}, bf16[2,512,2048]{2,1,0:T(8,128)(2,1)}, u32[]{:S(2)}) copy-start(bf16[2,512,2048]{2,1,0:T(8,128)(2,1)} %out_ref.1) | copy-start | bytes 12582916
  155.8 79.5 %copy-start.5 = (bf16[256,256]{1,0:T(8,128)(2,1)S(1)}, bf16[256,256]{1,0:T(8,128)(2,1)}, u32[]{:S(2)}) copy-start(bf16[256,256]{1,0:T(8,128)(2,1)} %get-tuple-element.24.code_ref) | copy-start | bytes 393220
